TPU v7x, 256 devices: a whole 4x4x8 slice. The times are simulated.
256 devices in a mesh: expert: 32 (over z, x), dp: 8 (over y, core).
Axes of the slice: x: 4, y: 4, z: 8, core: 2. Of those that a mesh axis runs over, the one named last changes fastest.
Arguments:
- tokens: bfloat16 [4096, 4096], P('expert', 'dp'), may hold values from -6 to 6
- out_grad: bfloat16 [4096, 4096], P('expert', 'dp'), may hold values from -6 to 6
- routes: int32 [4096, 4], P('expert'), may hold values from 0 to 31, all different within a row; in each aligned block of 128 rows (0 to 127, 128 to 255, ...) at most 18 rows name the same one
- gate_weights: float32 [4096, 4], P('expert'), may hold values from 0.05 to 0.5
- previous_home: int32 [32], replicated, may hold values from 0 to 31, each once
- next_home: int32 [32], replicated, may hold values from 0 to 31, each once
- w_in: bfloat16 [32, 2, 4096, 1024], P('expert', None, None, 'dp'), may hold values from -0.09375 to 0.09375
- w_out: bfloat16 [32, 1024, 4096], P('expert', 'dp'), may hold values from -0.1875 to 0.1875
- first_moment: float32 [32, 1024, 4096], P('expert', 'dp'), may hold values from -12 to 12
- second_moment: float32 [32, 1024, 4096], P('expert', 'dp'), may hold values from 1 to 30
Outputs:
- token_grad: bfloat16 [4096, 4096], P('expert', 'dp')
- new_first: float32 [32, 1024, 4096], P('expert', 'dp')
- new_second: float32 [32, 1024, 4096], P('expert', 'dp')
- adam_step: bfloat16 [32, 1024, 4096], P('expert', 'dp')
Inputs may be any that keep to these rules, and one draw needn't show every extreme that they name: `routes`: in each device's block of 128 tokens at most 18 pairs name the same expert, and some block reaches 18. `previous_home`: each expert appears once. `next_home`: each expert appears once.
All inputs are finite; a program needn't handle non-finite values.
Results may differ from a plain program's by a relative error of at most 0.0064.
Values may be sent and summed in bfloat16 or wider, within the bound.
A program may use at most 128 MiB of HBM per device.

v0:
```python
import jax
import jax.numpy as jnp
from jax import lax
from jax.sharding import PartitionSpec as P

beta_one = 0.9
beta_two = 0.95
epsilon = 1e-08


def relocate_moments(first_array, second_array, source):
    flat_first = first_array.reshape(1, -1)
    flat_second = second_array.reshape(1, -1)
    spread_first, spread_second = (
        lax.all_to_all(flat_first, "expert", split_axis=1, concat_axis=0, tiled=True),
        lax.all_to_all(flat_second, "expert", split_axis=1, concat_axis=0, tiled=True),
    )
    moved_first = jnp.take(spread_first, source, axis=0)
    moved_second = jnp.take(spread_second, source, axis=0)
    back_first, back_second = (
        lax.all_to_all(moved_first, "expert", split_axis=0, concat_axis=1, tiled=True),
        lax.all_to_all(moved_second, "expert", split_axis=0, concat_axis=1, tiled=True),
    )
    return (back_first.reshape(first_array.shape), back_second.reshape(second_array.shape))


def per_device(
    tokens,
    out_grad,
    routes,
    gate_weights,
    previous_home,
    next_home,
    w_in,
    w_out,
    first_moment,
    second_moment,
):
    devices = lax.axis_size("expert")
    tok_count = routes.shape[0]
    top_count = routes.shape[1]
    experts = previous_home.shape[0]
    capacity = tok_count * top_count * 9 // (8 * experts)
    slot_total = devices * capacity
    width = w_out.shape[2]
    device_index = jnp.arange(devices, dtype=jnp.int32)
    matched = (next_home[:, None] == device_index[None, :]).astype(jnp.int32)
    source = jnp.sum(matched * previous_home[:, None], axis=0)
    weight_in, weight_out = (w_in, w_out)
    moment_first, moment_second = (first_moment, second_moment)
    onehot = (routes[:, :, None] == jnp.arange(experts, dtype=jnp.int32)[None, None, :]).astype(
        jnp.int32
    )
    onehot = onehot.reshape(tok_count * top_count, experts)
    before = jnp.cumsum(onehot, axis=0) - onehot
    slot_index = jnp.sum(before * onehot, axis=1)
    target = jnp.sum(onehot * previous_home[None, :], axis=1)
    position = target * capacity + slot_index

    def place_pairs(values):
        columns = values.shape[1]
        empty = jnp.zeros((slot_total, columns), values.dtype)
        return empty.at[position].set(values).reshape(devices, capacity, columns)

    full_tokens, full_grads = (
        lax.all_gather(tokens, "dp", axis=1, tiled=True),
        lax.all_gather(out_grad, "dp", axis=1, tiled=True),
    )
    columns = full_tokens.shape[1]
    send_rows = place_pairs(
        jnp.broadcast_to(full_tokens[:, None, :], (tok_count, top_count, columns)).reshape(
            tok_count * top_count, columns
        )
    )
    scaled = gate_weights[:, :, None] * full_grads[:, None, :].astype(jnp.float32)
    send_grads = place_pairs(
        scaled.astype(jnp.bfloat16).reshape(tok_count * top_count, full_grads.shape[1])
    )
    slot_rows, slot_grads = (
        lax.all_to_all(send_rows, "expert", split_axis=0, concat_axis=0, tiled=True),
        lax.all_to_all(send_grads, "expert", split_axis=0, concat_axis=0, tiled=True),
    )
    slot_rows = slot_rows.reshape(slot_total, width)
    slot_grads = slot_grads.reshape(slot_total, width)
    gate_in = weight_in[0, 0]
    up_in = weight_in[0, 1]
    out_rows = weight_out[0]
    gate_pre = jnp.dot(slot_rows, gate_in, preferred_element_type=jnp.float32)
    up_value = jnp.dot(slot_rows, up_in, preferred_element_type=jnp.float32)
    sigmoid_gate = jax.nn.sigmoid(gate_pre)
    silu_gate = gate_pre * sigmoid_gate
    activation = (silu_gate * up_value).astype(jnp.bfloat16)
    over_slots = (((0,), (0,)), ((), ()))
    over_columns = (((1,), (1,)), ((), ()))
    weight_grad = lax.dot_general(
        activation, slot_grads, over_slots, preferred_element_type=jnp.float32
    )
    act_grad = lax.dot_general(
        slot_grads, out_rows, over_columns, preferred_element_type=jnp.float32
    )
    gate_grad = (
        act_grad * up_value * sigmoid_gate * (1.0 + gate_pre * (1.0 - sigmoid_gate))
    ).astype(jnp.bfloat16)
    up_grad = (act_grad * silu_gate).astype(jnp.bfloat16)
    partial_value = lax.dot_general(
        gate_grad, gate_in, over_columns, preferred_element_type=jnp.float32
    )
    partial_value = partial_value + lax.dot_general(
        up_grad, up_in, over_columns, preferred_element_type=jnp.float32
    )
    returned = lax.all_to_all(
        partial_value.astype(jnp.bfloat16).reshape(devices, capacity, width),
        "expert",
        split_axis=0,
        concat_axis=0,
        tiled=True,
    )
    picked = jnp.take(returned.reshape(slot_total, width), position, axis=0).astype(jnp.float32)
    token_total = picked.reshape(tok_count, top_count, width).sum(axis=1)
    token_grad = lax.psum_scatter(token_total, "dp", scatter_dimension=1, tiled=True).astype(
        jnp.bfloat16
    )
    updated_first = beta_one * moment_first[0] + (1.0 - beta_one) * weight_grad
    updated_second = beta_two * moment_second[0] + (1.0 - beta_two) * weight_grad * weight_grad
    placed_first, placed_second = relocate_moments(
        updated_first[None], updated_second[None], source
    )
    adam_step = (placed_first / (jnp.sqrt(placed_second) + epsilon)).astype(jnp.bfloat16)
    return (token_grad, placed_first, placed_second, adam_step)


def solution(mesh):
    return jax.shard_map(
        per_device,
        mesh=mesh,
        in_specs=(
            P("expert", "dp"),
            P("expert", "dp"),
            P("expert", None),
            P("expert", None),
            P(),
            P(),
            P("expert", None, None, "dp"),
            P("expert", "dp", None),
            P("expert", "dp", None),
            P("expert", "dp", None),
        ),
        out_specs=(
            P("expert", "dp"),
            P("expert", "dp", None),
            P("expert", "dp", None),
            P("expert", "dp", None),
        ),
        check_vma=False,
    )
```

profile of v0, /device:TPU:2, one launch (start us, length us, event | category | flops | bytes accessed | tf_op | source)
XLA Modules:
  0.0 808.4 jit_solution(8281219123213261994)
XLA Ops:
  11.2 27.6 %all-gather.5.cloned.1.call-done = bf16[128,4096]{1,0:T(8,128)(2,1)} async-done(((bf16[128,512]{1,0:T(8,128)(2,1)}), bf16[128,4096]{1,0:T(8,128)(2,1)}) %all-gather.5.cloned.1.call-update) | async-done | bytes 1048592 | tf_op jit(solution)/shard_map/all_gather | solution.py:66
  51.0 10.5 %scatter_custom_fusion.1 = bf16[576,4096]{1,0:T(8,128)(2,1)} fusion(s32[512]{0:T(512)S(1)} %bitcast.55, bf16[512,4096]{1,0:T(8,128)(2,1)} %reshape.224, bf16[]{:T(256)} %constant.26.clone.1), kind=kCustom, calls=%fused_computation.11 | custom fusion | bytes 4719104 | tf_op jit(solution)/shard_map/scatter | solution.py:63
  61.5 7.6 reshape.182
  69.1 10.3 %all-to-all-start.1 = ((bf16[32,18,4096]{2,1,0:T(8,128)(2,1)}), bf16[32,18,4096]{2,1,0:T(8,128)(2,1)}, u32[]{:S(2)}, u32[]{:S(2)}) async-start(bf16[32,18,4096]{2,1,0:T(8,128)(2,1)} %reshape.182), calls=%async_computation.1 | async-start | bytes 12582912 | tf_op jit(solution)/shard_map/all_to_all | solution.py:80
  80.4 27.2 %all-gather.3.cloned.1.call-done = bf16[128,4096]{1,0:T(8,128)(2,1)} async-done(((bf16[128,512]{1,0:T(8,128)(2,1)}), bf16[128,4096]{1,0:T(8,128)(2,1)}) %all-gather.3.cloned.1.call-update) | async-done | bytes 1048592 | tf_op jit(solution)/shard_map/all_gather | solution.py:67
  114.4 10.0 %mul.117 = f32[512,4096]{1,0:T(8,128)} reshape(f32[128,4,4096]{2,1,0:T(4,128)} %mul.116) | data formatting | bytes 16777216 | tf_op jit(solution)/shard_map/mul | solution.py:75
  124.4 11.8 %scatter_custom_fusion = bf16[576,4096]{1,0:T(8,128)(2,1)} fusion(s32[512]{0:T(512)S(1)} %bitcast.56, f32[512,4096]{1,0:T(8,128)} %mul.117, f32[512]{0:T(512)S(1)} %mul.114, bf16[]{:T(256)} %constant.26.clone.1), kind=kCustom, calls=%fused_computation.8 | custom fusion | flops 4194304 | bytes 13109250 | tf_op jit(solution)/shard_map/scatter | solution.py:63
  143.7 79.8 %all-to-all-done.1 = bf16[32,18,4096]{2,1,0:T(8,128)(2,1)} async-done(((bf16[32,18,4096]{2,1,0:T(8,128)(2,1)}), bf16[32,18,4096]{2,1,0:T(8,128)(2,1)}, u32[]{:S(2)}, u32[]{:S(2)}) %all-to-all-start.1) | async-done | bytes 4718624 | tf_op jit(solution)/shard_map/all_to_all | solution.py:80
  223.5 10.7 %all-to-all-start = ((bf16[32,18,4096]{2,1,0:T(8,128)(2,1)}), bf16[32,18,4096]{2,1,0:T(8,128)(2,1)}, u32[]{:S(2)}, u32[]{:S(2)}) async-start(bf16[32,18,4096]{2,1,0:T(8,128)(2,1)} %reshape.179), calls=%async_computation | async-start | bytes 12582912 | tf_op jit(solution)/shard_map/all_to_all | solution.py:81
  234.3 7.9 reshape.183
  248.2 129.1 %all-to-all-done = bf16[32,18,4096]{2,1,0:T(8,128)(2,1)} async-done(((bf16[32,18,4096]{2,1,0:T(8,128)(2,1)}), bf16[32,18,4096]{2,1,0:T(8,128)(2,1)}, u32[]{:S(2)}, u32[]{:S(2)}) %all-to-all-start) | async-done | bytes 4718624 | tf_op jit(solution)/shard_map/all_to_all | solution.py:81
  377.3 7.7 reshape.180
  395.0 9.5 %all-to-all-start.3 = ((f32[1,32,16384]{2,0,1:T(1,128)}), f32[1,32,16384]{2,0,1:T(1,128)S(1)}, u32[]{:S(2)}, u32[]{:S(2)}) async-start(f32[1,32,16384]{2,0,1:T(1,128)} %all_to_all.66), calls=%async_computation.4 | async-start | bytes 4194304 | tf_op jit(solution)/shard_map/all_to_all | solution.py:15
  409.2 44.5 %all-to-all-done.3 = f32[1,32,16384]{2,0,1:T(1,128)S(1)} async-done(((f32[1,32,16384]{2,0,1:T(1,128)}), f32[1,32,16384]{2,0,1:T(1,128)S(1)}, u32[]{:S(2)}, u32[]{:S(2)}) %all-to-all-start.3) | async-done | bytes 2097184 | tf_op jit(solution)/shard_map/all_to_all | solution.py:15
  466.5 42.9 %all-to-all-done.5 = f32[1,32,16384]{2,0,1:T(1,128)} async-done(((f32[1,32,16384]{2,0,1:T(1,128)}), f32[1,32,16384]{2,0,1:T(1,128)}, u32[]{:S(2)}, u32[]{:S(2)}) %all-to-all-start.5) | async-done | bytes 2097184 | tf_op jit(solution)/shard_map/all_to_all | solution.py:16
  537.2 7.6 reshape.184
  544.8 31.5 %all-to-all-done.4 = f32[32,1,16384]{2,1,0:T(1,128)S(1)} async-done(((f32[32,1,16384]{2,1,0:T(1,128)}), f32[32,1,16384]{2,1,0:T(1,128)S(1)}, u32[]{:S(2)}, u32[]{:S(2)}) %all-to-all-start.4) | async-done | bytes 2097184 | tf_op jit(solution)/shard_map/all_to_all | solution.py:21
  588.2 130.4 %all-to-all-done.2 = bf16[32,18,4096]{2,1,0:T(8,128)(2,1)} async-done(((bf16[32,18,4096]{2,1,0:T(8,128)(2,1)}), bf16[32,18,4096]{2,1,0:T(8,128)(2,1)}, u32[]{:S(2)}, u32[]{:S(2)}) %all-to-all-start.2) | async-done | bytes 4718624 | tf_op jit(solution)/shard_map/all_to_all | solution.py:111
  718.6 7.7 all-to-all-start.6
  726.6 7.8 reshape.185
  734.4 11.5 %gather_fusion = bf16[512,4096]{1,0:T(8,128)(2,1)} fusion(bf16[576,4096]{1,0:T(8,128)(2,1)} %reshape.185, s32[1024]{0:T(1024)S(1)} %pad_clamp_fusion.1), kind=kCustom, calls=%fused_computation.2 | custom fusion | bytes 8390656 | tf_op jit(solution)/shard_map/jit(_take)/gather | solution.py:118
  753.3 11.3 %convert_reduce_fusion = f32[128,4096]{1,0:T(8,128)} fusion(bf16[128,4,4096]{2,1,0:T(4,128)(2,1)} %gather.10, pred[128,4]{1,0:T(8,128)(4,1)S(1)} %compare_and_fusion), kind=kLoop, calls=%fused_computation.6 | loop fusion | flops 5767168 | bytes 6291968 | tf_op jit(solution)/shard_map/reduce_sum | solution.py:119
  775.0 8.1 %reduce.2 = f32[32,16384]{1,0:T(8,128)} reduce(f32[32,1,16384]{2,1,0:T(1,128)} %all-to-all-done.6, f32[]{:T(128)} %constant.58), dimensions={1}, to_apply=%all_to_all.65.reduce_sub_computation | reduce | bytes 4194308 | tf_op jit(solution)/shard_map/all_to_all | solution.py:22
  789.2 10.8 %reduce-scatter.2.cloned.1.call-done = f32[128,512]{1,0:T(8,128)} async-done(((f32[128,4096]{1,0:T(8,128)}), f32[128,512]{1,0:T(8,128)}) %reduce-scatter.2.cloned.1.call-update) | async-done | bytes 262160 | tf_op jit(solution)/shard_map/reduce_scatter | solution.py:120
  (75 shorter events, 130.3 us)
Async XLA Ops:
  7.2 521.2 %copy-start = (bf16[1,128,4096]{2,1,0:T(8,128)(2,1)S(1)}, bf16[1,128,4096]{2,1,0:T(8,128)(2,1)}, u32[]{:S(2)}) copy-start(bf16[1,128,4096]{2,1,0:T(8,128)(2,1)} %param.19) | copy-start | bytes 3145732
  7.2 31.6 %all-gather.5.cloned.1.call-start = ((), (), s32[]{:S(2)}) async-start(), calls=%async_computation.9 | async-start | bytes 1179648 | tf_op jit(solution)/shard_map/all_gather | solution.py:66
  69.1 11.1 %copy-start.7 = (f32[128,4]{0,1:T(4,128)S(1)}, f32[128,4]{0,1:T(4,128)}, u32[]{:S(2)}) copy-start(f32[128,4]{0,1:T(4,128)} %param.15) | copy-start | bytes 6148
  69.1 154.4 %all-to-all-start.1 = ((bf16[32,18,4096]{2,1,0:T(8,128)(2,1)}), bf16[32,18,4096]{2,1,0:T(8,128)(2,1)}, u32[]{:S(2)}, u32[]{:S(2)}) async-start(bf16[32,18,4096]{2,1,0:T(8,128)(2,1)} %reshape.182), calls=%async_computation.1 | async-start | bytes 12582912 | tf_op jit(solution)/shard_map/all_to_all | solution.py:80
  79.4 28.2 %all-gather.3.cloned.1.call-start = ((), (), s32[]{:S(2)}) async-start(), calls=%async_computation.8 | async-start | bytes 1179648 | tf_op jit(solution)/shard_map/all_gather | solution.py:67
  223.5 153.8 %all-to-all-start = ((bf16[32,18,4096]{2,1,0:T(8,128)(2,1)}), bf16[32,18,4096]{2,1,0:T(8,128)(2,1)}, u32[]{:S(2)}, u32[]{:S(2)}) async-start(bf16[32,18,4096]{2,1,0:T(8,128)(2,1)} %reshape.179), calls=%async_computation | async-start | bytes 12582912 | tf_op jit(solution)/shard_map/all_to_all | solution.py:81
  234.3 8.0 copy-start.4
  242.2 3.9 copy-start.3
  395.0 58.7 %all-to-all-start.3 = ((f32[1,32,16384]{2,0,1:T(1,128)}), f32[1,32,16384]{2,0,1:T(1,128)S(1)}, u32[]{:S(2)}, u32[]{:S(2)}) async-start(f32[1,32,16384]{2,0,1:T(1,128)} %all_to_all.66), calls=%async_computation.4 | async-start | bytes 4194304 | tf_op jit(solution)/shard_map/all_to_all | solution.py:15
  404.5 56.5 %copy-start.8 = (s32[32]{0:T(128)S(1)}, s32[32]{0:T(128)}, u32[]{:S(2)}) copy-start(s32[32]{0:T(128)} %param.16) | copy-start | bytes 388
  404.5 56.5 %copy-start.9 = (s32[32]{0:T(128)S(1)}, s32[32]{0:T(128)}, u32[]{:S(2)}) copy-start(s32[32]{0:T(128)} %param.17) | copy-start | bytes 388
  453.7 7.4 copy-start.2
  453.7 55.7 %all-to-all-start.5 = ((f32[1,32,16384]{2,0,1:T(1,128)}), f32[1,32,16384]{2,0,1:T(1,128)}, u32[]{:S(2)}, u32[]{:S(2)}) async-start(f32[1,32,16384]{2,0,1:T(1,128)} %all_to_all.67), calls=%async_computation.6 | async-start | bytes 4194304 | tf_op jit(solution)/shard_map/all_to_all | solution.py:16
  522.0 54.3 %all-to-all-start.4 = ((f32[32,1,16384]{2,1,0:T(1,128)}), f32[32,1,16384]{2,1,0:T(1,128)S(1)}, u32[]{:S(2)}, u32[]{:S(2)}) async-start(f32[32,1,16384]{2,1,0:T(1,128)} %copy.31), calls=%async_computation.5 | async-start | bytes 4194304 | tf_op jit(solution)/shard_map/all_to_all | solution.py:21
  528.4 3.9 copy-start.5
  528.4 3.9 copy-start.6
  576.3 142.3 %all-to-all-start.2 = ((bf16[32,18,4096]{2,1,0:T(8,128)(2,1)}), bf16[32,18,4096]{2,1,0:T(8,128)(2,1)}, u32[]{:S(2)}, u32[]{:S(2)}) async-start(bf16[32,18,4096]{2,1,0:T(8,128)(2,1)} %reshape.184), calls=%async_computation.2 | async-start | bytes 12582912 | tf_op jit(solution)/shard_map/all_to_all | solution.py:111
  718.6 56.3 %all-to-all-start.6 = ((f32[32,1,16384]{2,1,0:T(1,128)}), f32[32,1,16384]{2,1,0:T(1,128)}, u32[]{:S(2)}, u32[]{:S(2)}) async-start(f32[32,1,16384]{2,1,0:T(1,128)} %copy.33), calls=%async_computation.7 | async-start | bytes 4194304 | tf_op jit(solution)/shard_map/all_to_all | solution.py:22
  726.4 73.7 %reduce-scatter.2.cloned.1.call-start = ((), (), s32[]{:S(2)}) async-start(), calls=%async_computation.10 | async-start | bytes 2359296 | tf_op jit(solution)/shard_map/reduce_scatter | solution.py:120
  773.7 12.2 %copy-start.1 = (f32[1,128,4096]{2,1,0:T(8,128)}, f32[1,128,4096]{2,1,0:T(8,128)S(1)}, u32[]{:S(2)}) copy-start(f32[1,128,4096]{2,1,0:T(8,128)S(1)} %reshape.186) | copy-start | bytes 6291460
Sparse Core Ops, SparseCore 0:
  9.9 28.8 all-gather.4
  82.1 25.4 all-gather.2
  764.7 35.3 reduce-scatter.1
where the time goes:
time: 819 us; the launch traced here: 808 us
  waiting for transfers between devices  526 us (64%)
  local copies, waits for them, and re-layouts  138 us (17%)
  starting transfers between devices  59.4 us (7%)
  other arithmetic  49.4 us (6%)
  matrix products  21.2 us (3%)
  between operations  14.3 us (2%)
    all_to_all x1, waiting for transfers between devices, per_device(): lax.all_to_all(partial_value.astype(jnp.bfloat16).reshape(devices, capaci...  130 us
    all_to_all x1, waiting for transfers between devices, per_device(): lax.all_to_all(send_grads, 'expert', split_axis=0, concat_axis=0, tiled=T...  129 us
    all_to_all x1, waiting for transfers between devices, per_device(): lax.all_to_all(send_rows, 'expert', split_axis=0, concat_axis=0, tiled=True)  79.8 us
    all_to_all x1, waiting for transfers between devices, relocate_moments(): lax.all_to_all(flat_first, 'expert', split_axis=1, concat_axis=0, tiled=T...  44.5 us
    all_to_all x1, waiting for transfers between devices, relocate_moments(): lax.all_to_all(flat_second, 'expert', split_axis=1, concat_axis=0, tiled=...  42.9 us
    all_to_all x1, waiting for transfers between devices, relocate_moments(): lax.all_to_all(moved_first, 'expert', split_axis=0, concat_axis=1, tiled=...  31.5 us
    all_gather x1, waiting for transfers between devices, per_device(): lax.all_gather(tokens, 'dp', axis=1, tiled=True)  27.6 us
    all_gather x1, waiting for transfers between devices, per_device(): lax.all_gather(out_grad, 'dp', axis=1, tiled=True)  27.2 us
  transfers between devices with their start and end apart: 10, of which 10 were waited for; matrix products, arithmetic and copies ran while one was open for 18% of the time, Pallas kernels for 0%

commit v1 on v0

v1 whole, which is shorter than its diff:
```python
import jax
import jax.numpy as jnp
from jax import lax
from jax.sharding import PartitionSpec as P

beta_one = 0.9
beta_two = 0.95
epsilon = 1e-08


def per_device(
    tokens,
    out_grad,
    routes,
    gate_weights,
    previous_home,
    next_home,
    w_in,
    w_out,
    first_moment,
    second_moment,
):
    devices = lax.axis_size("expert")
    parts = lax.axis_size("dp")
    tok_count, top_count = routes.shape
    experts = previous_home.shape[0]
    capacity = tok_count * top_count * 9 // (8 * experts)
    slot_total = devices * capacity
    width = w_out.shape[2]
    hidden = w_out.shape[1]
    local = tokens.shape[1]
    piece = width // devices
    pairs = tok_count * top_count

    def across(values):
        return lax.all_to_all(values, "expert", split_axis=0, concat_axis=0, tiled=True)

    device_index = jnp.arange(devices, dtype=jnp.int32)
    matched = (next_home[:, None] == device_index[None, :]).astype(jnp.int32)
    source = jnp.sum(matched * previous_home[:, None], axis=0)

    both = jnp.stack([first_moment[0], second_moment[0]]).astype(jnp.bfloat16)
    both = both.reshape(2, hidden, devices, piece).transpose(2, 0, 1, 3)
    spread = across(both)

    flat = routes.reshape(pairs)
    onehot = flat[:, None] == jnp.arange(experts, dtype=jnp.int32)[None, :]
    order = jnp.arange(pairs, dtype=jnp.int32)
    lower = (order[None, :] < order[:, None]).astype(jnp.bfloat16)
    before = jnp.dot(lower, onehot.astype(jnp.bfloat16), preferred_element_type=jnp.float32)
    slot_index = jnp.sum(jnp.where(onehot, before, 0.0), axis=1).astype(jnp.int32)
    target = jnp.sum(jnp.where(onehot, previous_home[None, :], 0), axis=1)
    position = (target * capacity + slot_index).reshape(tok_count, top_count)
    hit = position[None] == jnp.arange(slot_total, dtype=jnp.int32)[:, None, None]
    place = jnp.any(hit, axis=2).astype(jnp.bfloat16)
    gate_of = jnp.sum(jnp.where(hit, gate_weights[None], 0.0), axis=(1, 2))

    send_rows = jnp.dot(place, tokens, preferred_element_type=jnp.float32)
    send_grads = jnp.dot(place, out_grad, preferred_element_type=jnp.float32) * gate_of[:, None]
    send = jnp.concatenate([send_rows, send_grads], axis=1).astype(jnp.bfloat16)
    here = across(send.reshape(devices, capacity, 2 * local)).reshape(slot_total, 2 * local)
    full = lax.all_gather(here, "dp", axis=0, tiled=False)

    def side(start):
        return full[:, :, start : start + local].transpose(1, 0, 2).reshape(slot_total, width)

    slot_rows, slot_grads = side(0), side(local)
    gate_in, up_in, out_rows = w_in[0, 0], w_in[0, 1], w_out[0]
    gate_pre = jnp.dot(slot_rows, gate_in, preferred_element_type=jnp.float32)
    up_value = jnp.dot(slot_rows, up_in, preferred_element_type=jnp.float32)
    sigmoid_gate = jax.nn.sigmoid(gate_pre)
    silu_gate = gate_pre * sigmoid_gate
    activation = (silu_gate * up_value).astype(jnp.bfloat16)
    over_columns = (((1,), (1,)), ((), ()))
    weight_grad = lax.dot_general(
        activation, slot_grads, (((0,), (0,)), ((), ())), preferred_element_type=jnp.float32
    )
    wg_spread = across(
        weight_grad.astype(jnp.bfloat16).reshape(hidden, devices, piece).transpose(1, 0, 2)
    )
    act_grad = lax.dot_general(
        slot_grads, out_rows, over_columns, preferred_element_type=jnp.float32
    )
    gate_grad = (
        act_grad * up_value * sigmoid_gate * (1.0 + gate_pre * (1.0 - sigmoid_gate))
    ).astype(jnp.bfloat16)
    up_grad = (act_grad * silu_gate).astype(jnp.bfloat16)
    partial_value = lax.dot_general(
        gate_grad, gate_in, over_columns, preferred_element_type=jnp.float32
    ) + lax.dot_general(up_grad, up_in, over_columns, preferred_element_type=jnp.float32)
    pieces = partial_value.astype(jnp.bfloat16).reshape(slot_total, parts, local).transpose(1, 0, 2)
    pieces = lax.all_to_all(pieces, "dp", split_axis=0, concat_axis=0, tiled=True)
    summed = jnp.sum(pieces.astype(jnp.float32), axis=0).astype(jnp.bfloat16)
    returned = across(summed.reshape(devices, capacity, local)).reshape(slot_total, local)
    token_grad = lax.dot_general(
        place, returned, (((0,), (0,)), ((), ())), preferred_element_type=jnp.float32
    ).astype(jnp.bfloat16)

    pick = (source[:, None] == device_index[None, :]).astype(jnp.bfloat16)
    held = jnp.tensordot(pick, spread, 1, preferred_element_type=jnp.float32)
    grad_piece = jnp.tensordot(pick, wg_spread, 1, preferred_element_type=jnp.float32)
    mid_first = beta_one * held[:, 0] + (1.0 - beta_one) * grad_piece
    mid_second = beta_two * held[:, 1] + (1.0 - beta_two) * grad_piece * grad_piece
    back = across(jnp.stack([mid_first, mid_second], axis=1).astype(jnp.bfloat16))
    back = back.transpose(1, 2, 0, 3).reshape(2, 1, hidden, width).astype(jnp.float32)
    new_first, new_second = back[0], back[1]
    adam_step = (new_first / (jnp.sqrt(new_second) + epsilon)).astype(jnp.bfloat16)
    return (token_grad, new_first, new_second, adam_step)


def solution(mesh):
    return jax.shard_map(
        per_device,
        mesh=mesh,
        in_specs=(
            P("expert", "dp"),
            P("expert", "dp"),
            P("expert", None),
            P("expert", None),
            P(),
            P(),
            P("expert", None, None, "dp"),
            P("expert", "dp", None),
            P("expert", "dp", None),
            P("expert", "dp", None),
        ),
        out_specs=(
            P("expert", "dp"),
            P("expert", "dp", None),
            P("expert", "dp", None),
            P("expert", "dp", None),
        ),
        check_vma=False,
    )
```

time: 819 us -> 344 us (0.42); the launches traced: 808 us -> 343 us
  waiting for transfers between devices: 526 us -> 176 us
  local copies, waits for them, and re-layouts: 138 us -> 41.1 us
  blocking collectives: 0 us -> 50.7 us
  other arithmetic: 49.4 us -> 11.4 us
  starting transfers between devices: 59.4 us -> 31.6 us
    all_to_all x7 -> x5, waiting for transfers between devices: 459 us -> 136 us  [the longest x4 85.9 us: across(): lax.all_to_all(values, 'expert', split_axis=0, concat_axis=0, tiled=True)]
    all_to_all x0 -> x1, blocking collectives: none -> 50.7 us  [across(): lax.all_to_all(values, 'expert', split_axis=0, concat_axis=0, tiled=True)]
    reshape x9 -> x6, local copies, waits for them, and re-layouts: 58 us -> 8.65 us  [the longest x2 3.59 us: side(): full[:, :, start:start + local].transpose(1, 0, 2)]
    all_to_all x7 -> x5, starting transfers between devices: 58.8 us -> 31.6 us  [the longest x4 27 us: across(): lax.all_to_all(values, 'expert', split_axis=0, concat_axis=0, tiled=True)]
    gather x4 -> x0, local copies, waits for them, and re-layouts: 23.8 us -> none  [the longest x2 18.9 us: per_device(): jnp.take(returned.reshape(slot_total, width), position, axis=0)]
    all_to_all x3 -> x0, other arithmetic: 19.2 us -> none  [the longest x2 12 us: relocate_moments(): lax.all_to_all(moved_second, 'expert', split_axis=0, concat_axis=1, tiled...]
    mul x3 -> x0, local copies, waits for them, and re-layouts: 16.9 us -> none  [per_device(): gate_weights[:, :, None] * full_grads[:, None, :].astype(jnp.float32)]
    all_gather x2 -> x1, waiting for transfers between devices: 54.8 us -> 39.7 us  [per_device(): full = lax.all_gather(here, 'dp', axis=0, tiled=False)]
  transfers between devices with their start and end apart: 10 -> 6, of which waited for: 10 -> 5; matrix products, arithmetic and copies ran while one was open for 18% -> 13% of each run, Pallas kernels for 0% -> 0%
where the time goes in v1:
time: 344 us; the launch traced here: 343 us
  waiting for transfers between devices  176 us (51%)
  blocking collectives  50.7 us (15%)
  local copies, waits for them, and re-layouts  41.1 us (12%)
  starting transfers between devices  31.6 us (9%)
  matrix products  17.3 us (5%)
  between operations  14.3 us (4%)
  other arithmetic  11.4 us (3%)
    all_to_all x4, waiting for transfers between devices, across(): lax.all_to_all(values, 'expert', split_axis=0, concat_axis=0, tiled=True)  85.9 us
    all_to_all x1, blocking collectives, across(): lax.all_to_all(values, 'expert', split_axis=0, concat_axis=0, tiled=True)  50.7 us
    all_to_all x1, waiting for transfers between devices, per_device(): lax.all_to_all(pieces, 'dp', split_axis=0, concat_axis=0, tiled=True)  50.5 us
    all_gather x1, waiting for transfers between devices, per_device(): full = lax.all_gather(here, 'dp', axis=0, tiled=False)  39.7 us
    all_to_all x4, starting transfers between devices, across(): lax.all_to_all(values, 'expert', split_axis=0, concat_axis=0, tiled=True)  27 us
    unnamed x25, local copies, waits for them, and re-layouts  20.2 us
  transfers between devices with their start and end apart: 6, of which 5 were waited for; matrix products, arithmetic and copies ran while one was open for 13% of the time, Pallas kernels for 0%

profile of v1, /device:TPU:2, one launch (start us, length us, event | category | flops | bytes accessed | tf_op | source)
XLA Modules:
  0.0 342.5 jit_solution(15987083593221111909)
XLA Ops:
  13.3 50.7 %all_to_all.30 = bf16[32,18,1024]{2,1,0:T(8,128)(2,1)S(1)} all-to-all(bf16[32,18,1024]{2,1,0:T(8,128)(2,1)S(1)} %copy.57), channel_id=1, replica_groups=mesh['expert'=32,'dp'=8] {'expert'}, dimensions={0} | all-to-all | bytes 2359296 | tf_op jit(solution)/shard_map/all_to_all | solution.py:36
  65.2 2.7 copy.62
  71.0 2.7 copy.63
  73.7 5.6 %all-to-all-start.3 = ((bf16[32,2,128,128]{3,2,1,0:T(8,128)(2,1)}), bf16[32,2,128,128]{3,2,1,0:T(8,128)(2,1)S(1)}, u32[]{:S(2)}, u32[]{:S(2)}) async-start(bf16[32,2,128,128]{3,2,1,0:T(8,128)(2,1)} %copy.63), calls=%async_computation.3 | async-start | bytes 4194304 | tf_op jit(solution)/shard_map/all_to_all | solution.py:36
  79.3 39.7 %all-gather.2.cloned.1.call-done = bf16[8,576,1024]{2,1,0:T(8,128)(2,1)} async-done(((bf16[1,576,1024]{2,1,0:T(8,128)(2,1)}), bf16[8,576,1024]{2,1,0:T(8,128)(2,1)}) %all-gather.2.cloned.1.call-update) | async-done | bytes 9437200 | tf_op jit(solution)/shard_map/all_gather | solution.py:62
  119.0 6.6 %slice_bitcast_fusion.1 = (bf16[8,72,8,512]{3,2,1,0:T(8,128)(2,1)S(1)}, bf16[8,72,8,512]{3,2,1,0:T(8,128)(2,1)}) fusion(bf16[8,576,1024]{2,1,0:T(8,128)(2,1)} %all-gather.2.cloned.1.call-done), kind=kLoop, calls=%fused_computation.4 | loop fusion | bytes 18874368
  125.6 2.9 copy.76
  138.0 2.6 copy.87
  140.5 4.6 %all-to-all-start.1 = ((bf16[8,576,512]{2,1,0:T(8,128)(2,1)}), bf16[8,576,512]{2,1,0:T(8,128)(2,1)}, u32[]{:S(2)}, u32[]{:S(2)}) async-start(bf16[8,576,512]{2,1,0:T(8,128)(2,1)} %bitcast.87), calls=%async_computation.1 | async-start | bytes 9437184 | tf_op jit(solution)/shard_map/all_to_all | solution.py:92
  145.1 3.5 %fusion.8 = bf16[16,32,8,128]{3,2,1,0:T(8,128)(2,1)S(1)} fusion(bf16[576,4096]{1,0:T(8,128)(2,1)} %bitcast.86, f32[576,128]{1,0:T(8,128)} %copy-done.5, f32[576,128]{1,0:T(8,128)S(1)} %fusion.16), kind=kOutput, calls=%fused_computation.21 | convolution fusion | flops 604946432 | bytes 6356992 | tf_op jit(solution)/shard_map/dot_general | solution.py:75
  149.9 50.5 %all-to-all-done.1 = bf16[8,576,512]{2,1,0:T(8,128)(2,1)} async-done(((bf16[8,576,512]{2,1,0:T(8,128)(2,1)}), bf16[8,576,512]{2,1,0:T(8,128)(2,1)}, u32[]{:S(2)}, u32[]{:S(2)}) %all-to-all-start.1) | async-done | bytes 4718624 | tf_op jit(solution)/shard_map/all_to_all | solution.py:92
  200.4 10.2 %all-to-all-start.4 = ((bf16[32,128,128]{2,1,0:T(8,128)(2,1)}), bf16[32,128,128]{2,1,0:T(8,128)(2,1)}, u32[]{:S(2)}, u32[]{:S(2)}) async-start(bf16[32,128,128]{2,1,0:T(8,128)(2,1)} %bitcast.93), calls=%async_computation.4 | async-start | bytes 2097152 | tf_op jit(solution)/shard_map/all_to_all | solution.py:36
  210.6 3.3 reduce_sum.51
  215.0 23.5 %all-to-all-done.4 = bf16[32,128,128]{2,1,0:T(8,128)(2,1)} async-done(((bf16[32,128,128]{2,1,0:T(8,128)(2,1)}), bf16[32,128,128]{2,1,0:T(8,128)(2,1)}, u32[]{:S(2)}, u32[]{:S(2)}) %all-to-all-start.4) | async-done | bytes 1048608 | tf_op jit(solution)/shard_map/all_to_all | solution.py:36
  238.5 5.6 %all-to-all-start.2 = ((bf16[32,18,512]{2,1,0:T(8,128)(2,1)}), bf16[32,18,512]{2,1,0:T(8,128)(2,1)S(1)}, u32[]{:S(2)}, u32[]{:S(2)}) async-start(bf16[32,18,512]{2,1,0:T(8,128)(2,1)} %reshape.115), calls=%async_computation.2 | async-start | bytes 1572864 | tf_op jit(solution)/shard_map/all_to_all | solution.py:36
  245.6 2.7 fusion.12
  248.5 2.1 copy.67
  250.6 14.6 %all-to-all-done.2 = bf16[32,18,512]{2,1,0:T(8,128)(2,1)S(1)} async-done(((bf16[32,18,512]{2,1,0:T(8,128)(2,1)}), bf16[32,18,512]{2,1,0:T(8,128)(2,1)S(1)}, u32[]{:S(2)}, u32[]{:S(2)}) %all-to-all-start.2) | async-done | bytes 589856 | tf_op jit(solution)/shard_map/all_to_all | solution.py:36
  265.2 5.6 %all-to-all-start.5 = ((bf16[32,2,128,128]{3,2,1,0:T(8,128)(2,1)}), bf16[32,2,128,128]{3,2,1,0:T(8,128)(2,1)}, u32[]{:S(2)}, u32[]{:S(2)}) async-start(bf16[32,2,128,128]{3,2,1,0:T(8,128)(2,1)} %copy.67), calls=%async_computation.5 | async-start | bytes 4194304 | tf_op jit(solution)/shard_map/all_to_all | solution.py:36
  272.0 47.8 %all-to-all-done.5 = bf16[32,2,128,128]{3,2,1,0:T(8,128)(2,1)} async-done(((bf16[32,2,128,128]{3,2,1,0:T(8,128)(2,1)}), bf16[32,2,128,128]{3,2,1,0:T(8,128)(2,1)}, u32[]{:S(2)}, u32[]{:S(2)}) %all-to-all-start.5) | async-done | bytes 2097184 | tf_op jit(solution)/shard_map/all_to_all | solution.py:36
  319.8 3.1 copy.68
  325.2 2.9 copy.69
  328.1 3.6 %divide_convert_fusion = bf16[1,128,4096]{1,2,0:T(8,128)(2,1)} fusion(f32[1,128,32,128]{1,3,2,0:T(8,128)S(1)} %get-tuple-element.16, f32[1,128,32,128]{1,3,2,0:T(8,128)} %get-tuple-element.17), kind=kLoop, calls=%fused_computation.19 | loop fusion | flops 1572864 | bytes 5242880 | tf_op jit(solution)/shard_map/convert_element_type | solution.py:107
  333.4 2.3 copy.71
  (56 shorter events, 28.9 us)
Async XLA Ops:
  7.2 122.0 %copy-start = (bf16[1,128,4096]{2,1,0:T(8,128)(2,1)S(1)}, bf16[1,128,4096]{2,1,0:T(8,128)(2,1)}, u32[]{:S(2)}) copy-start(bf16[1,128,4096]{2,1,0:T(8,128)(2,1)} %param.17) | copy-start | bytes 3145732
  7.2 111.8 %all-gather.2.cloned.1.call-start = ((), (), s32[]{:S(2)}) async-start(), calls=%async_computation.6 | async-start | bytes 10616832 | tf_op jit(solution)/shard_map/all_gather | solution.py:62
  8.2 3.9 %copy-start.6 = (bf16[128,512]{1,0:T(8,128)(2,1)S(1)}, bf16[128,512]{1,0:T(8,128)(2,1)}, u32[]{:S(2)}) copy-start(bf16[128,512]{1,0:T(8,128)(2,1)} %param.10) | copy-start | bytes 393220
  65.2 2.7 copy-start.4
  73.7 66.8 %all-to-all-start.3 = ((bf16[32,2,128,128]{3,2,1,0:T(8,128)(2,1)}), bf16[32,2,128,128]{3,2,1,0:T(8,128)(2,1)S(1)}, u32[]{:S(2)}, u32[]{:S(2)}) async-start(bf16[32,2,128,128]{3,2,1,0:T(8,128)(2,1)} %copy.63), calls=%async_computation.3 | async-start | bytes 4194304 | tf_op jit(solution)/shard_map/all_to_all | solution.py:36
  129.2 2.3 copy-start.2
  129.2 3.2 copy-start.3
  135.1 1.4 copy-start.5
  140.5 59.9 %all-to-all-start.1 = ((bf16[8,576,512]{2,1,0:T(8,128)(2,1)}), bf16[8,576,512]{2,1,0:T(8,128)(2,1)}, u32[]{:S(2)}, u32[]{:S(2)}) async-start(bf16[8,576,512]{2,1,0:T(8,128)(2,1)} %bitcast.87), calls=%async_computation.1 | async-start | bytes 9437184 | tf_op jit(solution)/shard_map/all_to_all | solution.py:92
  200.4 38.1 %all-to-all-start.4 = ((bf16[32,128,128]{2,1,0:T(8,128)(2,1)}), bf16[32,128,128]{2,1,0:T(8,128)(2,1)}, u32[]{:S(2)}, u32[]{:S(2)}) async-start(bf16[32,128,128]{2,1,0:T(8,128)(2,1)} %bitcast.93), calls=%async_computation.4 | async-start | bytes 2097152 | tf_op jit(solution)/shard_map/all_to_all | solution.py:36
  214.0 30.2 %copy-start.7 = (s32[32]{0:T(128)S(1)}, s32[32]{0:T(128)}, u32[]{:S(2)}) copy-start(s32[32]{0:T(128)} %param.14) | copy-start | bytes 388
  214.0 30.2 %copy-start.8 = (s32[32]{0:T(128)S(1)}, s32[32]{0:T(128)}, u32[]{:S(2)}) copy-start(s32[32]{0:T(128)} %param.15) | copy-start | bytes 388
  238.5 26.7 %all-to-all-start.2 = ((bf16[32,18,512]{2,1,0:T(8,128)(2,1)}), bf16[32,18,512]{2,1,0:T(8,128)(2,1)S(1)}, u32[]{:S(2)}, u32[]{:S(2)}) async-start(bf16[32,18,512]{2,1,0:T(8,128)(2,1)} %reshape.115), calls=%async_computation.2 | async-start | bytes 1572864 | tf_op jit(solution)/shard_map/all_to_all | solution.py:36
  265.2 54.6 %all-to-all-start.5 = ((bf16[32,2,128,128]{3,2,1,0:T(8,128)(2,1)}), bf16[32,2,128,128]{3,2,1,0:T(8,128)(2,1)}, u32[]{:S(2)}, u32[]{:S(2)}) async-start(bf16[32,2,128,128]{3,2,1,0:T(8,128)(2,1)} %copy.67), calls=%async_computation.5 | async-start | bytes 4194304 | tf_op jit(solution)/shard_map/all_to_all | solution.py:36
  331.6 4.1 %copy-start.1 = (bf16[1,128,4096]{2,1,0:T(8,128)(2,1)S(1)}, bf16[1,128,4096]{2,1,0:T(8,128)(2,1)}, u32[]{:S(2)}) copy-start(bf16[1,128,4096]{2,1,0:T(8,128)(2,1)} %param.17) | copy-start | bytes 3145732
Sparse Core Ops, SparseCore 0:
  65.3 53.5 all-gather.1

commit v2 on v1

v2 whole, which is shorter than its diff:
```python
import functools

import jax
import jax.numpy as jnp
from jax import lax
from jax.experimental import pallas as pl
from jax.experimental.pallas import tpu as pltpu
from jax.sharding import PartitionSpec as P

beta_one = 0.9
beta_two = 0.95
epsilon = 1e-08

NE = 32
NZ, NX = 8, 4
ND = 8
NY = 4
TOK = 128
TOP = 4
MAIN = 16
OVER = 2
LANE = 128
FEAT = 512
WIDTH = 4096
HID = 128
ROWS = NE * MAIN
EXTRA = NE * OVER
SLOTS = ROWS + EXTRA
PACK = 2 * FEAT + LANE
BACK = FEAT + LANE
BLOCK = NX * MAIN
F32 = jnp.float32
BF16 = jnp.bfloat16
MESH = pl.DeviceIdType.MESH
VMEM_LIMIT = 60 << 20


def iota(shape, dim):
    return lax.broadcasted_iota(jnp.int32, shape, dim)


def dot(a, b, dims=((1,), (0,))):
    return lax.dot_general(a, b, (dims, ((), ())), preferred_element_type=F32)


def prepare_kernel(
    home_ref, routes_ref, gates_ref, tok_ref, grad_ref, send_ref, main_ref, over_ref, code_x, gate_x
):
    routes = routes_ref[...]
    target = jnp.zeros_like(routes)
    for e in range(NE):
        target = jnp.where(routes == e, home_ref[e], target)
    dest = iota((NE, TOK), 0)
    chosen = jnp.zeros((NE, TOK), F32)
    gate = jnp.zeros((NE, TOK), F32)
    for k in range(TOP):
        same = target[k : k + 1, :] == dest
        chosen = jnp.where(same, 1.0, chosen)
        gate = jnp.where(same, gates_ref[k : k + 1, :], gate)
    earlier = jnp.where(iota((TOK, TOK), 0) < iota((TOK, TOK), 1), 1.0, 0.0).astype(BF16)
    count = dot(chosen.astype(BF16), earlier)
    code = jnp.where(chosen > 0.5, count, -1.0)
    for j in range(NE):
        rows = pl.ds(j * MAIN, MAIN)
        code_x[rows, :] = jnp.broadcast_to(code[j : j + 1, :], (MAIN, TOK))
        gate_x[rows, :] = jnp.broadcast_to(gate[j : j + 1, :], (MAIN, TOK))
    code = code_x[...]
    gate = gate_x[...]
    within = iota((ROWS, TOK), 0) % MAIN
    hit = code == within.astype(F32)
    place = jnp.where(hit, 1.0, 0.0).astype(BF16)
    scale = jnp.sum(jnp.where(hit, gate, 0.0), axis=1, keepdims=True)
    main_ref[...] = place
    send_ref[:, 0:FEAT] = dot(place, tok_ref[...]).astype(BF16)
    send_ref[:, FEAT : 2 * FEAT] = (dot(place, grad_ref[...]) * scale).astype(BF16)
    hit = code == (MAIN + within % OVER).astype(F32)
    scale = jnp.sum(jnp.where(hit, gate, 0.0), axis=1, keepdims=True)
    over_ref[...] = jnp.where(hit, 1.0, 0.0).astype(BF16)
    chunk = within // OVER
    packed = jnp.zeros((ROWS, LANE), F32)
    for c in range(8):
        part = jnp.where(hit & (chunk == c), 1.0, 0.0).astype(BF16)
        held = tok_ref if c < 4 else grad_ref
        packed = packed + dot(part, held[:, (c % 4) * LANE : (c % 4 + 1) * LANE])
    packed = jnp.where(chunk >= 4, packed * scale, packed)
    send_ref[:, 2 * FEAT : PACK] = packed.astype(BF16)


def main_kernel(
    source_ref,
    send_ref,
    first_hbm,
    second_hbm,
    win_hbm,
    wout_hbm,
    ret_ref,
    back_ref,
    g,
    first_v,
    second_v,
    wgu,
    wout,
    raw_s,
    raw_r,
    wg_s,
    wg_r,
    back_s,
    u,
    sib_r,
    pair,
    y_r,
    xt,
    xg,
    acc,
    agrad,
    act,
    act_t,
    gu,
    ret_s,
    sel,
    load_sem,
    own_sem,
    disp_ss,
    disp_rs,
    raw_ss,
    raw_rs,
    wg_ss,
    wg_rs,
    back_ss,
    back_rs,
    ret_ss,
    ret_rs,
    near_ss,
    near_rs,
    sib_ss,
    sib_rs,
    sum_ss,
    sum_rs,
    ysum_ss,
    ysum_rs,
):
    e = lax.axis_index("expert")
    d = lax.axis_index("dp")
    z, x = lax.div(e, NX), lax.rem(e, NX)
    y, c = lax.div(d, 2), lax.rem(d, 2)
    sib = y * 2 + 1 - c

    def dz_of(i):
        odd = i % 2
        return odd * ((i + 1) // 2) + (1 - odd) * ((NZ - i // 2) % NZ)

    def target(k):
        i, dx = lax.div(k, NX), lax.rem(k, NX)
        odd = lax.rem(i, 2)
        dz = odd * lax.div(i + 1, 2) + (1 - odd) * lax.rem(NZ - lax.div(i, 2), NZ)
        return lax.rem(z + dz, NZ) * NX + lax.rem(x + dx, NX)

    def y_of(step):
        return lax.rem(y + step + NY, NY) * 2 + c

    def loop(body, lower=1, upper=NE):
        def step(k, carry):
            body(k)
            return carry

        lax.fori_loop(lower, upper, step, 0)

    barrier = pltpu.get_barrier_semaphore()

    def greet(k):
        pl.semaphore_signal(barrier, inc=1, device_id=(target(k), d), device_id_type=MESH)

    loop(greet)
    for peer in (y_of(1), y_of(2), y_of(3), sib):
        pl.semaphore_signal(barrier, inc=1, device_id=(e, peer), device_id_type=MESH)

    loads = [
        pltpu.make_async_copy(first_hbm.at[0], first_v, load_sem.at[0]),
        pltpu.make_async_copy(second_hbm.at[0], second_v, load_sem.at[1]),
        pltpu.make_async_copy(win_hbm.at[0, 0], wgu.at[:, pl.ds(0, HID)], load_sem.at[2]),
        pltpu.make_async_copy(win_hbm.at[0, 1], wgu.at[:, pl.ds(HID, HID)], load_sem.at[3]),
        pltpu.make_async_copy(wout_hbm.at[0], wout, load_sem.at[4]),
    ]
    for load in loads:
        load.start()
    pl.semaphore_wait(barrier, NE - 1 + 4)

    def rows16(j):
        return pl.ds(pl.multiple_of(j * MAIN, MAIN), MAIN)

    def remote(src, dst, ss, rs, who):
        return pltpu.make_async_remote_copy(
            src_ref=src, dst_ref=dst, send_sem=ss, recv_sem=rs, device_id=who, device_id_type=MESH
        )

    def disp(k):
        to = target(k)
        return remote(
            send_ref.at[rows16(to)], g.at[d, rows16(e)], disp_ss.at[k], disp_rs.at[k], (to, d)
        )

    def raw(k):
        to = target(k)
        return remote(raw_s.at[to], raw_r.at[e], raw_ss.at[k], raw_rs.at[k], (to, d))

    def wg(k):
        to = target(k)
        return remote(wg_s.at[to], wg_r.at[e], wg_ss.at[k], wg_rs.at[k], (to, d))

    def back(k):
        to = target(k)
        return remote(back_s.at[to], back_ref.at[e], back_ss.at[k], back_rs.at[k], (to, d))

    def ret(k):
        to = target(k)
        return remote(
            ret_s.at[rows16(to)], ret_ref.at[rows16(e)], ret_ss.at[k], ret_rs.at[k], (to, d)
        )

    loop(lambda k: disp(k).start())
    own = [
        pltpu.make_async_copy(send_ref.at[rows16(e)], g.at[d, rows16(e)], own_sem.at[0]),
        pltpu.make_async_copy(raw_s.at[e], raw_r.at[e], own_sem.at[1]),
        pltpu.make_async_copy(wg_s.at[e], wg_r.at[e], own_sem.at[2]),
        pltpu.make_async_copy(back_s.at[e], back_ref.at[e], own_sem.at[3]),
        pltpu.make_async_copy(ret_s.at[rows16(e)], ret_ref.at[rows16(e)], own_sem.at[4]),
    ]
    own[0].start()

    loads[0].wait()
    loads[1].wait()

    def cut(j):
        cols = pl.ds(pl.multiple_of(j * LANE, LANE), LANE)
        raw_s[j, 0] = first_v[:, cols].astype(BF16)
        raw_s[j, 1] = second_v[:, cols].astype(BF16)

    loop(cut, 0)
    r, q = iota((ROWS, ROWS), 0), iota((ROWS, ROWS), 1)
    spot = (r % EXTRA) // OVER * MAIN + r // EXTRA * OVER + r % OVER
    sel[...] = jnp.where(q == spot, 1.0, 0.0).astype(BF16)

    def block(i):
        return pl.ds(pl.multiple_of(lax.rem(z + NZ - dz_of(i), NZ) * BLOCK, BLOCK), BLOCK)

    def near(way, hop, i):
        step = 1 if way == 0 else -1
        held = g.at[y_of(-step * hop), block(i)]
        n = (way * 2 + hop) * NZ + i
        return remote(held, held, near_ss.at[n], near_rs.at[n], (e, y_of(step)))

    def side(back_by, i):
        held = g.at[y_of(-back_by), block(i)]
        n = (back_by % NY) * NZ + i
        return remote(held, held, sib_ss.at[n], sib_rs.at[n], (e, sib))

    def from_near(i):
        near(0, 0, i).wait_recv()
        if i % 2 == 0:
            near(0, 1, i).start()
        side(1, i).start()
        near(1, 0, i).wait_recv()
        if i % 2 == 1:
            near(1, 1, i).start()
        side(3, i).start()

    def from_far(i):
        near(i % 2, 1, i).wait_recv()
        side(2, i).start()

    for i in range(NZ):
        for dx in range(NX):
            if i == 0 and dx == 0:
                own[0].wait()
            else:
                disp(jnp.int32(i * NX + dx)).wait_recv()
        near(0, 0, i).start()
        near(1, 0, i).start()
        side(0, i).start()
        if i >= 1:
            from_near(i - 1)
        if i >= 2:
            from_far(i - 2)
    loop(lambda k: raw(k).start())
    own[1].start()
    from_near(NZ - 1)
    from_far(NZ - 2)
    from_far(NZ - 1)
    for load in loads[2:]:
        load.wait()
    for i in range(NZ):
        for b in range(NY):
            side(b, i).wait_recv()

    def part(j):
        return pl.ds(pl.multiple_of(j * FEAT, FEAT), FEAT)

    def lanes(j):
        return pl.ds(pl.multiple_of(j * LANE, LANE), LANE)

    def unpack(j):
        moved = dot(sel[...], g[j, :, 2 * FEAT : PACK]).astype(BF16)
        for k in range(4):
            xt[:, lanes(j * 4 + k)] = moved[k * EXTRA : (k + 1) * EXTRA]
            xg[:, lanes(j * 4 + k)] = moved[(k + 4) * EXTRA : (k + 5) * EXTRA]

    loop(unpack, 0, ND)
    acc[...] = jnp.zeros_like(acc)
    agrad[...] = jnp.zeros_like(agrad)

    def forward(j):
        w = wgu[part(j), :]
        acc[0:ROWS] += dot(g[j, :, 0:FEAT], w)
        acc[ROWS:SLOTS] += dot(xt[:, part(j)], w)
        o = wout[:, part(j)]
        agrad[0:ROWS] += dot(g[j, :, FEAT : 2 * FEAT], o, ((1,), (1,)))
        agrad[ROWS:SLOTS] += dot(xg[:, part(j)], o, ((1,), (1,)))

    loop(forward, 0, ND)

    def pointwise(j):
        rows = pl.ds(pl.multiple_of(j * EXTRA, EXTRA), EXTRA)
        gate, up, ag = acc[rows, 0:HID], acc[rows, HID : 2 * HID], agrad[rows]
        sig = jax.nn.sigmoid(gate)
        silu = gate * sig
        act[rows] = silu * up
        gu[rows, 0:HID] = (ag * up * sig * (1.0 + gate * (1.0 - sig))).astype(BF16)
        gu[rows, HID : 2 * HID] = (ag * silu).astype(BF16)

    loop(pointwise, 0, SLOTS // EXTRA)
    act_t[...] = act[...].T.astype(BF16)

    def outer(j):
        w = dot(act_t[:, 0:ROWS], g[j, :, FEAT : 2 * FEAT])
        w = w + dot(act_t[:, ROWS:SLOTS], xg[:, part(j)])
        for k in range(4):
            wg_s[j * 4 + k] = w[:, k * LANE : (k + 1) * LANE].astype(BF16)

    loop(outer, 0, ND)
    loop(lambda k: wg(k).start())
    own[2].start()

    def share(j):
        u[j] = dot(gu[...], wgu[part(j), :], ((1,), (1,))).astype(BF16)

    def to_sib(j):
        return remote(u.at[j * 2 + 1 - c], sib_r.at[j], sum_ss.at[j], sum_rs.at[j], (e, sib))

    def shares_out(j):
        share(j * 2 + 1 - c)
        to_sib(j).start()

    loop(shares_out, 0, NY)
    loop(lambda j: share(j * 2 + c), 0, NY)

    def to_y(o):
        return remote(
            pair.at[o], y_r.at[o], ysum_ss.at[o], ysum_rs.at[o], (e, lax.rem(y + o, NY) * 2 + c)
        )

    loop(lambda j: to_sib(j).wait_recv(), 0, NY)
    for o in (1, 3, 2, 0):
        ty = lax.rem(y + o, NY)
        pair[o] = (u[ty * 2 + c].astype(F32) + sib_r[ty].astype(F32)).astype(BF16)
        if o:
            to_y(o).start()

    own[1].wait()
    own[2].wait()
    loop(lambda k: raw(k).wait_recv())
    loop(lambda k: wg(k).wait_recv())

    def update(to):
        j = source_ref[to]
        w = wg_r[j].astype(F32)
        back_s[to, 0] = (beta_one * raw_r[j, 0].astype(F32) + (1.0 - beta_one) * w).astype(BF16)
        back_s[to, 1] = (
            beta_two * raw_r[j, 1].astype(F32) + (1.0 - beta_two) * w * w
        ).astype(BF16)

    def send_back(k):
        update(target(k))
        back(k).start()

    loop(send_back)
    update(e)
    own[3].start()

    for o in (1, 3, 2):
        to_y(o).wait_recv()

    def total(rows):
        value = pair[0, rows].astype(F32)
        for o in (1, 2, 3):
            value = value + y_r[o, rows].astype(F32)
        return value.astype(BF16)

    def add(j):
        rows = pl.ds(pl.multiple_of(j * EXTRA, EXTRA), EXTRA)
        ret_s[rows, 0:FEAT] = total(rows)

    loop(add, 0, ROWS // EXTRA)
    rest = total(pl.ds(ROWS, EXTRA))
    packed = jnp.zeros((ROWS, LANE), F32)
    for k in range(4):
        packed = packed + dot(
            sel[k * EXTRA : (k + 1) * EXTRA, :],
            rest[:, k * LANE : (k + 1) * LANE],
            ((0,), (0,)),
        )
    ret_s[:, FEAT:BACK] = packed.astype(BF16)
    loop(lambda k: ret(k).start())
    own[4].start()

    loop(lambda k: disp(k).wait_send())
    loop(lambda k: raw(k).wait_send())
    loop(lambda k: wg(k).wait_send())
    for i in range(NZ):
        near(0, 0, i).wait_send()
        near(1, 0, i).wait_send()
        near(i % 2, 1, i).wait_send()
        for b in range(NY):
            side(b, i).wait_send()
    loop(lambda j: to_sib(j).wait_send(), 0, NY)
    loop(lambda o: to_y(o).wait_send(), 1, NY)
    own[3].wait()
    loop(lambda k: back(k).wait())
    own[4].wait()
    loop(lambda k: ret(k).wait())


def finish_kernel(back_ref, ret_ref, main_ref, over_ref, tok_ref, first_ref, second_ref, step_ref):
    for k in range(4):
        cols = slice(k * LANE, (k + 1) * LANE)
        one, two = back_ref[k, 0].astype(F32), back_ref[k, 1].astype(F32)
        first_ref[0, :, cols] = one
        second_ref[0, :, cols] = two
        step_ref[0, :, cols] = (one / (jnp.sqrt(two) + epsilon)).astype(BF16)

    @pl.when(pl.program_id(0) == 0)
    def _():
        total = dot(main_ref[...], ret_ref[:, 0:FEAT], ((0,), (0,)))
        chunk = iota((ROWS, TOK), 0) % MAIN // OVER
        for k in range(4):
            cols = slice(k * LANE, (k + 1) * LANE)
            part = jnp.where(chunk == k, over_ref[...].astype(F32), 0.0).astype(BF16)
            more = dot(part, ret_ref[:, FEAT:BACK], ((0,), (0,)))
            tok_ref[:, cols] = (total[:, cols] + more).astype(BF16)


def per_device(
    tokens,
    out_grad,
    routes,
    gate_weights,
    previous_home,
    next_home,
    w_in,
    w_out,
    first_moment,
    second_moment,
):
    device_index = jnp.arange(NE, dtype=jnp.int32)
    matched = (next_home[:, None] == device_index[None, :]).astype(jnp.int32)
    source = jnp.sum(matched * previous_home[:, None], axis=0)

    vmem = pl.BlockSpec(memory_space=pltpu.VMEM)
    smem = pl.BlockSpec(memory_space=pltpu.SMEM)
    anywhere = pl.BlockSpec(memory_space=pl.ANY)
    shape = jax.ShapeDtypeStruct
    send, place_main, place_over = pl.pallas_call(
        prepare_kernel,
        out_shape=(
            shape((ROWS, PACK), BF16),
            shape((ROWS, TOK), BF16),
            shape((ROWS, TOK), BF16),
        ),
        in_specs=[smem, vmem, vmem, vmem, vmem],
        out_specs=(vmem, vmem, vmem),
        scratch_shapes=[pltpu.VMEM((ROWS, TOK), F32), pltpu.VMEM((ROWS, TOK), F32)],
        compiler_params=pltpu.CompilerParams(vmem_limit_bytes=32 << 20),
        cost_estimate=pl.CostEstimate(flops=3 * 10**8, bytes_accessed=2 << 20, transcendentals=0),
        name="prepare",
    )(previous_home, routes.T, gate_weights.T, tokens, out_grad)

    dma = pltpu.SemaphoreType.DMA
    ret, back = pl.pallas_call(
        main_kernel,
        out_shape=(shape((ROWS, BACK), BF16), shape((NE, 2, HID, LANE), BF16)),
        in_specs=[smem, vmem, anywhere, anywhere, anywhere, anywhere],
        out_specs=(vmem, vmem),
        scratch_shapes=[
            pltpu.VMEM((ND, ROWS, PACK), BF16),
            pltpu.VMEM((HID, WIDTH), F32),
            pltpu.VMEM((HID, WIDTH), F32),
            pltpu.VMEM((WIDTH, 2 * HID), BF16),
            pltpu.VMEM((HID, WIDTH), BF16),
            pltpu.VMEM((NE, 2, HID, LANE), BF16),
            pltpu.VMEM((NE, 2, HID, LANE), BF16),
            pltpu.VMEM((NE, HID, LANE), BF16),
            pltpu.VMEM((NE, HID, LANE), BF16),
            pltpu.VMEM((NE, 2, HID, LANE), BF16),
            pltpu.VMEM((ND, SLOTS, FEAT), BF16),
            pltpu.VMEM((NY, SLOTS, FEAT), BF16),
            pltpu.VMEM((NY, SLOTS, FEAT), BF16),
            pltpu.VMEM((NY, SLOTS, FEAT), BF16),
            pltpu.VMEM((EXTRA, WIDTH), BF16),
            pltpu.VMEM((EXTRA, WIDTH), BF16),
            pltpu.VMEM((SLOTS, 2 * HID), F32),
            pltpu.VMEM((SLOTS, HID), F32),
            pltpu.VMEM((SLOTS, HID), F32),
            pltpu.VMEM((HID, SLOTS), BF16),
            pltpu.VMEM((SLOTS, 2 * HID), BF16),
            pltpu.VMEM((ROWS, BACK), BF16),
            pltpu.VMEM((ROWS, ROWS), BF16),
            dma((5,)),
            dma((5,)),
        ]
        + [dma((NE,))] * 14
        + [dma((NY,))] * 4,
        compiler_params=pltpu.CompilerParams(
            collective_id=0, has_side_effects=True, vmem_limit_bytes=VMEM_LIMIT
        ),
        cost_estimate=pl.CostEstimate(
            flops=4 * 10**9, bytes_accessed=16 << 20, transcendentals=1 << 17
        ),
        name="exchange",
    )(source, send, first_moment, second_moment, w_in, w_out)

    steps = 8
    span = WIDTH // steps
    whole = lambda s: pl.BlockSpec(s, lambda i: (0,) * len(s))
    wide = pl.BlockSpec((1, HID, span), lambda i: (0, 0, i))
    return pl.pallas_call(
        finish_kernel,
        grid=(steps,),
        out_shape=(
            shape((TOK, FEAT), BF16),
            shape((1, HID, WIDTH), F32),
            shape((1, HID, WIDTH), F32),
            shape((1, HID, WIDTH), BF16),
        ),
        in_specs=[
            pl.BlockSpec((NE // steps, 2, HID, LANE), lambda i: (i, 0, 0, 0)),
            whole((ROWS, BACK)),
            whole((ROWS, TOK)),
            whole((ROWS, TOK)),
        ],
        out_specs=(whole((TOK, FEAT)), wide, wide, wide),
        compiler_params=pltpu.CompilerParams(vmem_limit_bytes=32 << 20),
        cost_estimate=pl.CostEstimate(
            flops=3 * 10**8, bytes_accessed=8 << 20, transcendentals=1 << 19
        ),
        name="finish",
    )(back, ret, place_main, place_over)


def solution(mesh):
    return jax.shard_map(
        per_device,
        mesh=mesh,
        in_specs=(
            P("expert", "dp"),
            P("expert", "dp"),
            P("expert", None),
            P("expert", None),
            P(),
            P(),
            P("expert", None, None, "dp"),
            P("expert", "dp", None),
            P("expert", "dp", None),
            P("expert", "dp", None),
        ),
        out_specs=(
            P("expert", "dp"),
            P("expert", "dp", None),
            P("expert", "dp", None),
            P("expert", "dp", None),
        ),
        check_vma=False,
    )
```

time: 344 us -> 213 us (0.62)
  Pallas kernels: 0 us -> 199 us
  waiting for transfers between devices: 176 us -> 0 us
  blocking collectives: 50.7 us -> 0 us
  local copies, waits for them, and re-layouts: 41.1 us -> 7.5 us
  starting transfers between devices: 31.6 us -> 0 us
  matrix products: 17.3 us -> 0 us
  between operations: 14.3 us -> 0.67 us
  other arithmetic: 11.4 us -> 1.27 us
    pallas_call x0 -> x3, Pallas kernels: none -> 199 us  [the longest x1 193 us: per_device(): pl.pallas_call(main_kernel, out_shape=(shape((ROWS, BACK), BF16), shape((...]
    all_to_all x5 -> x0, waiting for transfers between devices: 136 us -> none  [the longest x4 85.9 us: across(): lax.all_to_all(values, 'expert', split_axis=0, concat_axis=0, tiled=True)]
    all_to_all x1 -> x0, blocking collectives: 50.7 us -> none  [across(): lax.all_to_all(values, 'expert', split_axis=0, concat_axis=0, tiled=True)]
    all_gather x1 -> x0, waiting for transfers between devices: 39.7 us -> none  [per_device(): full = lax.all_gather(here, 'dp', axis=0, tiled=False)]
    all_to_all x5 -> x0, starting transfers between devices: 31.6 us -> none  [the longest x4 27 us: across(): lax.all_to_all(values, 'expert', split_axis=0, concat_axis=0, tiled=True)]
    dot_general x12 -> x0, matrix products: 17.3 us -> none  [the longest x1 3.49 us: per_device(): lax.dot_general(activation, slot_grads, (((0,), (0,)), ((), ())), preferr...]
    unnamed x25 -> x16, local copies, waits for them, and re-layouts: 20.2 us -> 7.5 us
    reshape x6 -> x0, local copies, waits for them, and re-layouts: 8.65 us -> none  [the longest x2 3.59 us: side(): full[:, :, start:start + local].transpose(1, 0, 2)]
  transfers between devices with their start and end apart: 6 -> 0, of which waited for: 5 -> 0; matrix products, arithmetic and copies ran while one was open for 13% -> 0% of each run, Pallas kernels for 0% -> 0%
where the time goes in v2:
time: 213 us; the launch traced here: 209 us
  Pallas kernels  199 us (93%)
  local copies, waits for them, and re-layouts  7.5 us (4%)
    pallas_call x1, Pallas kernels, per_device(): pl.pallas_call(main_kernel, out_shape=(shape((ROWS, BACK), BF16), shape((...  193 us
    unnamed x16, local copies, waits for them, and re-layouts  7.5 us
    pallas_call x1, Pallas kernels, per_device(): pl.pallas_call(finish_kernel, grid=(steps,), out_shape=(shape((TOK, FEAT)...  4.58 us

profile of v2, /device:TPU:2, one launch (start us, length us, event | category | flops | bytes accessed | tf_op | source)
XLA Modules:
  0.0 208.9 jit_solution(10053530081724315475)
XLA Ops:
  0.6 1.3 select_reduce_fusion.source_ref
  1.9 0.0 copy-start.2
  1.9 0.9 copy-done.2
  2.8 0.0 copy-start.3
  2.8 0.9 copy-done.3
  3.7 0.0 copy-start.4
  3.7 0.7 copy-done.4
  4.4 0.0 copy-start.5
  4.4 0.7 copy-done.5
  5.1 0.0 copy-start.6
  5.1 0.7 copy-done.6
  5.7 1.4 prepare.1
  7.2 0.0 copy-start.7
  7.2 1.0 copy-done.7
  8.2 193.4 %exchange.1 = (bf16[512,640]{1,0:T(8,128)(2,1)}, bf16[32,2,128,128]{3,2,1,0:T(8,128)(2,1)}) custom-call(s32[32]{0:T(128)} %select_reduce_fusion.source_ref, bf16[512,1152]{1,0:T(8,128)(2,1)} %copy-done.7, f32[1,128,4096]{2,1,0:T(8,128)} %first_hbm.1, f32[1,128,4096]{2,1,0:T(8,128)} %second_hbm.1, bf16[1,2,4096,128]{3,2,1,0:T(8,128)(2,1)} %win_hbm.1, ...), custom_call_target="tpu_custom_call" | custom-call | flops 4000000000 | bytes 16777216 | tf_op jit(solution)/shard_map/exchange/pallas_call | solution.py:487
  201.6 0.0 copy-start
  201.7 1.6 copy-done
  203.2 0.0 copy-start.1
  203.2 1.1 copy-done.1
  204.3 4.6 %finish.1 = (bf16[128,512]{1,0:T(8,128)(2,1)}, f32[1,128,4096]{2,1,0:T(8,128)}, f32[1,128,4096]{2,1,0:T(8,128)}, bf16[1,128,4096]{2,1,0:T(8,128)(2,1)}) custom-call(bf16[32,2,128,128]{3,2,1,0:T(8,128)(2,1)S(1)} %copy-done, bf16[512,640]{1,0:T(8,128)(2,1)S(1)} %copy-done.1, bf16[512,128]{1,0:T(8,128)(2,1)S(1)} %get-tuple-element.12.main_ref, ...), custom_call_target="tpu_custom_call" | custom-call | flops 300000000 | bytes 8388608 | tf_op jit(solution)/shard_map/finish/pallas_call | solution.py:534
Async XLA Ops:
  1.9 0.9 copy-start.2
  2.8 0.9 copy-start.3
  3.7 0.7 copy-start.4
  4.4 0.7 copy-start.5
  5.1 0.7 copy-start.6
  7.2 1.0 copy-start.7
  201.6 1.6 copy-start
  203.2 1.1 copy-start.1

commit v3 on v2

--- a/solution.py
+++ b/solution.py
@@ -29,6 +29,11 @@
 PACK = 2 * FEAT + LANE
 BACK = FEAT + LANE
 BLOCK = NX * MAIN
+RAW = 112
+POST = 2 * HID - RAW
+RAW_AT = 3
+RAW_N = 8
+LEAD = 5
 F32 = jnp.float32
 BF16 = jnp.bfloat16
 MESH = pl.DeviceIdType.MESH
@@ -43,7 +48,7 @@
     return lax.dot_general(a, b, (dims, ((), ())), preferred_element_type=F32)
 
 
-def prepare_kernel(
+def prepare(
     home_ref, routes_ref, gates_ref, tok_ref, grad_ref, send_ref, main_ref, over_ref, code_x, gate_x
 ):
     routes = routes_ref[...]
@@ -87,14 +92,27 @@
 
 
 def main_kernel(
-    source_ref,
-    send_ref,
+    previous_ref,
+    next_ref,
+    routes_hbm,
+    gates_hbm,
+    tok_hbm,
+    grad_hbm,
     first_hbm,
     second_hbm,
     win_hbm,
     wout_hbm,
     ret_ref,
     back_ref,
+    main_ref,
+    over_ref,
+    routes_v,
+    gates_v,
+    tok_v,
+    grad_v,
+    send_ref,
+    code_x,
+    gate_x,
     g,
     first_v,
     second_v,
@@ -181,8 +199,28 @@
         pltpu.make_async_copy(win_hbm.at[0, 1], wgu.at[:, pl.ds(HID, HID)], load_sem.at[3]),
         pltpu.make_async_copy(wout_hbm.at[0], wout, load_sem.at[4]),
     ]
-    for load in loads:
+    early = [
+        pltpu.make_async_copy(routes_hbm, routes_v, load_sem.at[5]),
+        pltpu.make_async_copy(gates_hbm, gates_v, load_sem.at[6]),
+        pltpu.make_async_copy(tok_hbm, tok_v, load_sem.at[7]),
+        pltpu.make_async_copy(grad_hbm, grad_v, load_sem.at[8]),
+    ]
+    for load in early + loads:
         load.start()
+    for load in early:
+        load.wait()
+    prepare(
+        previous_ref,
+        routes_v,
+        gates_v,
+        tok_v,
+        grad_v,
+        send_ref,
+        main_ref,
+        over_ref,
+        code_x,
+        gate_x,
+    )
     pl.semaphore_wait(barrier, NE - 1 + 4)
 
     def rows16(j):
@@ -217,7 +255,7 @@
             ret_s.at[rows16(to)], ret_ref.at[rows16(e)], ret_ss.at[k], ret_rs.at[k], (to, d)
         )
 
-    loop(lambda k: disp(k).start())
+    loop(lambda k: disp(k).start(), 1, LEAD * NX)
     own = [
         pltpu.make_async_copy(send_ref.at[rows16(e)], g.at[d, rows16(e)], own_sem.at[0]),
         pltpu.make_async_copy(raw_s.at[e], raw_r.at[e], own_sem.at[1]),
@@ -232,8 +270,8 @@
 
     def cut(j):
         cols = pl.ds(pl.multiple_of(j * LANE, LANE), LANE)
-        raw_s[j, 0] = first_v[:, cols].astype(BF16)
-        raw_s[j, 1] = second_v[:, cols].astype(BF16)
+        raw_s[j, 0] = first_v[0:RAW, cols].astype(BF16)
+        raw_s[j, 1] = second_v[0:RAW, cols].astype(BF16)
 
     loop(cut, 0)
     r, q = iota((ROWS, ROWS), 0), iota((ROWS, ROWS), 1)
@@ -268,29 +306,30 @@
         near(i % 2, 1, i).wait_recv()
         side(2, i).start()
 
-    for i in range(NZ):
-        for dx in range(NX):
-            if i == 0 and dx == 0:
+    sent = 1
+    for i in range(NZ + 2):
+        if i < NZ:
+            if i == 0:
                 own[0].wait()
-            else:
-                disp(jnp.int32(i * NX + dx)).wait_recv()
-        near(0, 0, i).start()
-        near(1, 0, i).start()
-        side(0, i).start()
-        if i >= 1:
+            loop(lambda k: disp(k).wait_recv(), max(1, i * NX), (i + 1) * NX)
+            near(0, 0, i).start()
+            near(1, 0, i).start()
+            side(0, i).start()
+            if i + LEAD < NZ:
+                loop(lambda k: disp(k).start(), (i + LEAD) * NX, (i + LEAD + 1) * NX)
+        if 1 <= i <= NZ:
             from_near(i - 1)
         if i >= 2:
             from_far(i - 2)
-    loop(lambda k: raw(k).start())
+        if i >= RAW_AT and sent < NE:
+            more = min(NE, sent + RAW_N)
+            loop(lambda k: raw(k).start(), sent, more)
+            sent = more
+    if sent < NE:
+        loop(lambda k: raw(k).start(), sent, NE)
     own[1].start()
-    from_near(NZ - 1)
-    from_far(NZ - 2)
-    from_far(NZ - 1)
     for load in loads[2:]:
         load.wait()
-    for i in range(NZ):
-        for b in range(NY):
-            side(b, i).wait_recv()
 
     def part(j):
         return pl.ds(pl.multiple_of(j * FEAT, FEAT), FEAT)
@@ -304,7 +343,6 @@
             xt[:, lanes(j * 4 + k)] = moved[k * EXTRA : (k + 1) * EXTRA]
             xg[:, lanes(j * 4 + k)] = moved[(k + 4) * EXTRA : (k + 5) * EXTRA]
 
-    loop(unpack, 0, ND)
     acc[...] = jnp.zeros_like(acc)
     agrad[...] = jnp.zeros_like(agrad)
 
@@ -316,7 +354,19 @@
         agrad[0:ROWS] += dot(g[j, :, FEAT : 2 * FEAT], o, ((1,), (1,)))
         agrad[ROWS:SLOTS] += dot(xg[:, part(j)], o, ((1,), (1,)))
 
-    loop(forward, 0, ND)
+    def origin(by, core):
+        j = lax.rem(y + by, NY) * 2 + core
+        unpack(j)
+        forward(j)
+
+    loop(lambda by: origin(by, c), 0, NY)
+    for i in range(NZ):
+        for b in (0, 1, 3):
+            side(b, i).wait_recv()
+    loop(lambda by: origin(by, 1 - c), NY - 1, NY + 2)
+    for i in range(NZ):
+        side(2, i).wait_recv()
+    origin(2, 1 - c)
 
     def pointwise(j):
         rows = pl.ds(pl.multiple_of(j * EXTRA, EXTRA), EXTRA)
@@ -334,11 +384,24 @@
         w = dot(act_t[:, 0:ROWS], g[j, :, FEAT : 2 * FEAT])
         w = w + dot(act_t[:, ROWS:SLOTS], xg[:, part(j)])
         for k in range(4):
-            wg_s[j * 4 + k] = w[:, k * LANE : (k + 1) * LANE].astype(BF16)
-
-    loop(outer, 0, ND)
-    loop(lambda k: wg(k).start())
+            n = j * 4 + k
+            piece = w[:, k * LANE : (k + 1) * LANE]
+            wg_s[n, 0:RAW] = piece[0:RAW].astype(BF16)
+            one, two = first_v[RAW:HID, lanes(n)], second_v[RAW:HID, lanes(n)]
+            piece = piece[RAW:HID]
+            wg_s[n, RAW:HID] = (beta_one * one + (1.0 - beta_one) * piece).astype(BF16)
+            wg_s[n, HID:POST] = (beta_two * two + (1.0 - beta_two) * piece * piece).astype(BF16)
+
+    outer(z)
+    loop(lambda k: wg(k).start(), 1, NX)
     own[2].start()
+
+    def outward(i):
+        outer(lax.div(target(i * NX), NX))
+        for dx in range(NX):
+            wg(i * NX + dx).start()
+
+    loop(outward, 1, NZ)
 
     def share(j):
         u[j] = dot(gu[...], wgu[part(j), :], ((1,), (1,))).astype(BF16)
@@ -371,12 +434,15 @@
     loop(lambda k: wg(k).wait_recv())
 
     def update(to):
-        j = source_ref[to]
-        w = wg_r[j].astype(F32)
-        back_s[to, 0] = (beta_one * raw_r[j, 0].astype(F32) + (1.0 - beta_one) * w).astype(BF16)
-        back_s[to, 1] = (
-            beta_two * raw_r[j, 1].astype(F32) + (1.0 - beta_two) * w * w
-        ).astype(BF16)
+        j = jnp.int32(0)
+        for n in range(NE):
+            j = j + jnp.where(next_ref[n] == to, previous_ref[n], 0)
+        w = wg_r[j, 0:RAW].astype(F32)
+        one, two = raw_r[j, 0].astype(F32), raw_r[j, 1].astype(F32)
+        back_s[to, 0, 0:RAW] = (beta_one * one + (1.0 - beta_one) * w).astype(BF16)
+        back_s[to, 1, 0:RAW] = (beta_two * two + (1.0 - beta_two) * w * w).astype(BF16)
+        back_s[to, 0, RAW:HID] = wg_r[j, RAW:HID]
+        back_s[to, 1, RAW:HID] = wg_r[j, HID:POST]
 
     def send_back(k):
         update(target(k))
@@ -460,45 +526,38 @@
     first_moment,
     second_moment,
 ):
-    device_index = jnp.arange(NE, dtype=jnp.int32)
-    matched = (next_home[:, None] == device_index[None, :]).astype(jnp.int32)
-    source = jnp.sum(matched * previous_home[:, None], axis=0)
-
     vmem = pl.BlockSpec(memory_space=pltpu.VMEM)
     smem = pl.BlockSpec(memory_space=pltpu.SMEM)
     anywhere = pl.BlockSpec(memory_space=pl.ANY)
     shape = jax.ShapeDtypeStruct
-    send, place_main, place_over = pl.pallas_call(
-        prepare_kernel,
+    dma = pltpu.SemaphoreType.DMA
+    ret, back, place_main, place_over = pl.pallas_call(
+        main_kernel,
         out_shape=(
-            shape((ROWS, PACK), BF16),
+            shape((ROWS, BACK), BF16),
+            shape((NE, 2, HID, LANE), BF16),
             shape((ROWS, TOK), BF16),
             shape((ROWS, TOK), BF16),
         ),
-        in_specs=[smem, vmem, vmem, vmem, vmem],
-        out_specs=(vmem, vmem, vmem),
-        scratch_shapes=[pltpu.VMEM((ROWS, TOK), F32), pltpu.VMEM((ROWS, TOK), F32)],
-        compiler_params=pltpu.CompilerParams(vmem_limit_bytes=32 << 20),
-        cost_estimate=pl.CostEstimate(flops=3 * 10**8, bytes_accessed=2 << 20, transcendentals=0),
-        name="prepare",
-    )(previous_home, routes.T, gate_weights.T, tokens, out_grad)
-
-    dma = pltpu.SemaphoreType.DMA
-    ret, back = pl.pallas_call(
-        main_kernel,
-        out_shape=(shape((ROWS, BACK), BF16), shape((NE, 2, HID, LANE), BF16)),
-        in_specs=[smem, vmem, anywhere, anywhere, anywhere, anywhere],
-        out_specs=(vmem, vmem),
+        in_specs=[smem, smem] + [anywhere] * 8,
+        out_specs=(vmem,) * 4,
         scratch_shapes=[
+            pltpu.VMEM((TOP, TOK), jnp.int32),
+            pltpu.VMEM((TOP, TOK), F32),
+            pltpu.VMEM((TOK, FEAT), BF16),
+            pltpu.VMEM((TOK, FEAT), BF16),
+            pltpu.VMEM((ROWS, PACK), BF16),
+            pltpu.VMEM((ROWS, TOK), F32),
+            pltpu.VMEM((ROWS, TOK), F32),
             pltpu.VMEM((ND, ROWS, PACK), BF16),
             pltpu.VMEM((HID, WIDTH), F32),
             pltpu.VMEM((HID, WIDTH), F32),
             pltpu.VMEM((WIDTH, 2 * HID), BF16),
             pltpu.VMEM((HID, WIDTH), BF16),
-            pltpu.VMEM((NE, 2, HID, LANE), BF16),
-            pltpu.VMEM((NE, 2, HID, LANE), BF16),
-            pltpu.VMEM((NE, HID, LANE), BF16),
-            pltpu.VMEM((NE, HID, LANE), BF16),
+            pltpu.VMEM((NE, 2, RAW, LANE), BF16),
+            pltpu.VMEM((NE, 2, RAW, LANE), BF16),
+            pltpu.VMEM((NE, POST, LANE), BF16),
+            pltpu.VMEM((NE, POST, LANE), BF16),
             pltpu.VMEM((NE, 2, HID, LANE), BF16),
             pltpu.VMEM((ND, SLOTS, FEAT), BF16),
             pltpu.VMEM((NY, SLOTS, FEAT), BF16),
@@ -513,7 +572,7 @@
             pltpu.VMEM((SLOTS, 2 * HID), BF16),
             pltpu.VMEM((ROWS, BACK), BF16),
             pltpu.VMEM((ROWS, ROWS), BF16),
-            dma((5,)),
+            dma((9,)),
             dma((5,)),
         ]
         + [dma((NE,))] * 14
@@ -525,7 +584,18 @@
             flops=4 * 10**9, bytes_accessed=16 << 20, transcendentals=1 << 17
         ),
         name="exchange",
-    )(source, send, first_moment, second_moment, w_in, w_out)
+    )(
+        previous_home,
+        next_home,
+        routes.T,
+        gate_weights.T,
+        tokens,
+        out_grad,
+        first_moment,
+        second_moment,
+        w_in,
+        w_out,
+    )
 
     steps = 8
     span = WIDTH // steps
@@ -547,7 +617,7 @@
             whole((ROWS, TOK)),
         ],
         out_specs=(whole((TOK, FEAT)), wide, wide, wide),
-        compiler_params=pltpu.CompilerParams(vmem_limit_bytes=32 << 20),
+        compiler_params=pltpu.CompilerParams(vmem_limit_bytes=VMEM_LIMIT),
         cost_estimate=pl.CostEstimate(
             flops=3 * 10**8, bytes_accessed=8 << 20, transcendentals=1 << 19
         ),

time: 213 us -> 182 us (0.85); the launches traced: 209 us -> 182 us
  Pallas kernels: 199 us -> 181 us
  local copies, waits for them, and re-layouts: 7.5 us -> 0 us
    pallas_call x1, Pallas kernels: 193 us -> 174 us  [per_device(): pl.pallas_call(main_kernel, out_shape=(shape((ROWS, BACK), BF16), shape((...]
    unnamed x16 -> x0, local copies, waits for them, and re-layouts: 7.5 us -> none
    pallas_call x1, Pallas kernels: 4.58 us -> 7.38 us  [per_device(): pl.pallas_call(finish_kernel, grid=(steps,), out_shape=(shape((TOK, FEAT)...]
where the time goes in v3:
time: 182 us
  Pallas kernels  181 us (99%)
    pallas_call x1, Pallas kernels, per_device(): pl.pallas_call(main_kernel, out_shape=(shape((ROWS, BACK), BF16), shape((...  174 us
    pallas_call x1, Pallas kernels, per_device(): pl.pallas_call(finish_kernel, grid=(steps,), out_shape=(shape((TOK, FEAT)...  7.38 us

profile of v3, /device:TPU:2, one launch (start us, length us, event | category | flops | bytes accessed | tf_op | source)
XLA Modules:
  0.0 181.8 jit_solution(14681674464216456110)
XLA Ops:
  0.6 173.7 %exchange.1 = (bf16[512,640]{1,0:T(8,128)(2,1)}, bf16[32,2,128,128]{3,2,1,0:T(8,128)(2,1)}, bf16[512,128]{1,0:T(8,128)(2,1)}, bf16[512,128]{1,0:T(8,128)(2,1)}) custom-call(s32[32]{0:T(128)} %previous_ref.1, s32[32]{0:T(128)} %next_ref.1, s32[4,128]{1,0:T(4,128)} %bitcast.2, f32[4,128]{1,0:T(4,128)} %bitcast.3, bf16[128,512]{1,0:T(8,128)(2,1)} %tok_hbm.1, ...), custom_call_target="tpu_custom_call" | custom-call | flops 4000000000 | bytes 16777216 | tf_op jit(solution)/shard_map/exchange/pallas_call | solution.py:534
  174.4 7.4 %finish.1 = (bf16[128,512]{1,0:T(8,128)(2,1)}, f32[1,128,4096]{2,1,0:T(8,128)}, f32[1,128,4096]{2,1,0:T(8,128)}, bf16[1,128,4096]{2,1,0:T(8,128)(2,1)}) custom-call(bf16[32,2,128,128]{3,2,1,0:T(8,128)(2,1)} %get-tuple-element.8.back_ref, bf16[512,640]{1,0:T(8,128)(2,1)} %get-tuple-element.9.ret_ref, bf16[512,128]{1,0:T(8,128)(2,1)} %get-tuple-element.10.main_ref, ...), custom_call_target="tpu_custom_call" | custom-call | flops 300000000 | bytes 8388608 | tf_op jit(solution)/shard_map/finish/pallas_call | solution.py:604

commit v4 on v3

--- a/solution.py
+++ b/solution.py
@@ -29,8 +29,9 @@
 PACK = 2 * FEAT + LANE
 BACK = FEAT + LANE
 BLOCK = NX * MAIN
-RAW = 112
-POST = 2 * HID - RAW
+HALF = HID // 2
+RAW = 48
+POST = 2 * HALF - RAW
 RAW_AT = 3
 RAW_N = 8
 LEAD = 5
@@ -121,7 +122,8 @@
     raw_s,
     raw_r,
     wg_s,
-    wg_r,
+    wg_r0,
+    wg_r1,
     back_s,
     u,
     sib_r,
@@ -162,6 +164,7 @@
     z, x = lax.div(e, NX), lax.rem(e, NX)
     y, c = lax.div(d, 2), lax.rem(d, 2)
     sib = y * 2 + 1 - c
+    wg_r = (wg_r0, wg_r1)
 
     def dz_of(i):
         odd = i % 2
@@ -241,13 +244,13 @@
         to = target(k)
         return remote(raw_s.at[to], raw_r.at[e], raw_ss.at[k], raw_rs.at[k], (to, d))
 
-    def wg(k):
-        to = target(k)
-        return remote(wg_s.at[to], wg_r.at[e], wg_ss.at[k], wg_rs.at[k], (to, d))
-
-    def back(k):
-        to = target(k)
-        return remote(back_s.at[to], back_ref.at[e], back_ss.at[k], back_rs.at[k], (to, d))
+    def wg(h, k):
+        to, n = target(k), h * NE + k
+        return remote(wg_s.at[h, to], wg_r[h].at[e], wg_ss.at[n], wg_rs.at[n], (to, d))
+
+    def back(h, k):
+        to, n = target(k), h * NE + k
+        return remote(back_s.at[h, to], back_ref.at[h, e], back_ss.at[n], back_rs.at[n], (to, d))
 
     def ret(k):
         to = target(k)
@@ -259,9 +262,11 @@
     own = [
         pltpu.make_async_copy(send_ref.at[rows16(e)], g.at[d, rows16(e)], own_sem.at[0]),
         pltpu.make_async_copy(raw_s.at[e], raw_r.at[e], own_sem.at[1]),
-        pltpu.make_async_copy(wg_s.at[e], wg_r.at[e], own_sem.at[2]),
-        pltpu.make_async_copy(back_s.at[e], back_ref.at[e], own_sem.at[3]),
+        pltpu.make_async_copy(wg_s.at[0, e], wg_r[0].at[e], own_sem.at[2]),
+        pltpu.make_async_copy(back_s.at[0, e], back_ref.at[0, e], own_sem.at[3]),
         pltpu.make_async_copy(ret_s.at[rows16(e)], ret_ref.at[rows16(e)], own_sem.at[4]),
+        pltpu.make_async_copy(wg_s.at[1, e], wg_r[1].at[e], own_sem.at[5]),
+        pltpu.make_async_copy(back_s.at[1, e], back_ref.at[1, e], own_sem.at[6]),
     ]
     own[0].start()
 
@@ -270,8 +275,10 @@
 
     def cut(j):
         cols = pl.ds(pl.multiple_of(j * LANE, LANE), LANE)
-        raw_s[j, 0] = first_v[0:RAW, cols].astype(BF16)
-        raw_s[j, 1] = second_v[0:RAW, cols].astype(BF16)
+        for h in range(2):
+            rows = slice(h * HALF, h * HALF + RAW)
+            raw_s[j, 0, h] = first_v[rows, cols].astype(BF16)
+            raw_s[j, 1, h] = second_v[rows, cols].astype(BF16)
 
     loop(cut, 0)
     r, q = iota((ROWS, ROWS), 0), iota((ROWS, ROWS), 1)
@@ -386,22 +393,27 @@
         for k in range(4):
             n = j * 4 + k
             piece = w[:, k * LANE : (k + 1) * LANE]
-            wg_s[n, 0:RAW] = piece[0:RAW].astype(BF16)
-            one, two = first_v[RAW:HID, lanes(n)], second_v[RAW:HID, lanes(n)]
-            piece = piece[RAW:HID]
-            wg_s[n, RAW:HID] = (beta_one * one + (1.0 - beta_one) * piece).astype(BF16)
-            wg_s[n, HID:POST] = (beta_two * two + (1.0 - beta_two) * piece * piece).astype(BF16)
+            for h in range(2):
+                wg_s[h, n, 0:RAW] = piece[h * HALF : h * HALF + RAW].astype(BF16)
+                rows = slice(h * HALF + RAW, (h + 1) * HALF)
+                one, two, p = first_v[rows, lanes(n)], second_v[rows, lanes(n)], piece[rows]
+                one = beta_one * one + (1.0 - beta_one) * p
+                two = beta_two * two + (1.0 - beta_two) * p * p
+                wg_s[h, n, RAW:HALF] = one.astype(BF16)
+                wg_s[h, n, HALF:POST] = two.astype(BF16)
 
     outer(z)
-    loop(lambda k: wg(k).start(), 1, NX)
+    loop(lambda k: wg(0, k).start(), 1, NX)
     own[2].start()
 
     def outward(i):
         outer(lax.div(target(i * NX), NX))
         for dx in range(NX):
-            wg(i * NX + dx).start()
+            wg(0, i * NX + dx).start()
 
     loop(outward, 1, NZ)
+    loop(lambda k: wg(1, k).start())
+    own[5].start()
 
     def share(j):
         u[j] = dot(gu[...], wgu[part(j), :], ((1,), (1,))).astype(BF16)
@@ -429,28 +441,32 @@
             to_y(o).start()
 
     own[1].wait()
-    own[2].wait()
     loop(lambda k: raw(k).wait_recv())
-    loop(lambda k: wg(k).wait_recv())
-
-    def update(to):
+
+    def update(h, to):
         j = jnp.int32(0)
         for n in range(NE):
             j = j + jnp.where(next_ref[n] == to, previous_ref[n], 0)
-        w = wg_r[j, 0:RAW].astype(F32)
-        one, two = raw_r[j, 0].astype(F32), raw_r[j, 1].astype(F32)
-        back_s[to, 0, 0:RAW] = (beta_one * one + (1.0 - beta_one) * w).astype(BF16)
-        back_s[to, 1, 0:RAW] = (beta_two * two + (1.0 - beta_two) * w * w).astype(BF16)
-        back_s[to, 0, RAW:HID] = wg_r[j, RAW:HID]
-        back_s[to, 1, RAW:HID] = wg_r[j, HID:POST]
-
-    def send_back(k):
-        update(target(k))
-        back(k).start()
-
-    loop(send_back)
-    update(e)
-    own[3].start()
+        w = wg_r[h][j, 0:RAW].astype(F32)
+        one, two = raw_r[j, 0, h].astype(F32), raw_r[j, 1, h].astype(F32)
+        one = beta_one * one + (1.0 - beta_one) * w
+        two = beta_two * two + (1.0 - beta_two) * w * w
+        back_s[h, to, 0, 0:RAW] = one.astype(BF16)
+        back_s[h, to, 1, 0:RAW] = two.astype(BF16)
+        back_s[h, to, 0, RAW:HALF] = wg_r[h][j, RAW:HALF]
+        back_s[h, to, 1, RAW:HALF] = wg_r[h][j, HALF:POST]
+
+    for h in range(2):
+        own[2 + 3 * h].wait()
+        loop(lambda k: wg(h, k).wait_recv())
+
+        def send_back(k):
+            update(h, target(k))
+            back(h, k).start()
+
+        loop(send_back)
+        update(h, e)
+        own[3 + 3 * h].start()
 
     for o in (1, 3, 2):
         to_y(o).wait_recv()
@@ -480,7 +496,8 @@
 
     loop(lambda k: disp(k).wait_send())
     loop(lambda k: raw(k).wait_send())
-    loop(lambda k: wg(k).wait_send())
+    for h in range(2):
+        loop(lambda k: wg(h, k).wait_send())
     for i in range(NZ):
         near(0, 0, i).wait_send()
         near(1, 0, i).wait_send()
@@ -489,19 +506,22 @@
             side(b, i).wait_send()
     loop(lambda j: to_sib(j).wait_send(), 0, NY)
     loop(lambda o: to_y(o).wait_send(), 1, NY)
-    own[3].wait()
-    loop(lambda k: back(k).wait())
+    for h in range(2):
+        own[3 + 3 * h].wait()
+        loop(lambda k: back(h, k).wait())
     own[4].wait()
     loop(lambda k: ret(k).wait())
 
 
 def finish_kernel(back_ref, ret_ref, main_ref, over_ref, tok_ref, first_ref, second_ref, step_ref):
-    for k in range(4):
-        cols = slice(k * LANE, (k + 1) * LANE)
-        one, two = back_ref[k, 0].astype(F32), back_ref[k, 1].astype(F32)
-        first_ref[0, :, cols] = one
-        second_ref[0, :, cols] = two
-        step_ref[0, :, cols] = (one / (jnp.sqrt(two) + epsilon)).astype(BF16)
+    for h in range(2):
+        rows = slice(h * HALF, (h + 1) * HALF)
+        for k in range(4):
+            cols = slice(k * LANE, (k + 1) * LANE)
+            one, two = back_ref[h, k, 0].astype(F32), back_ref[h, k, 1].astype(F32)
+            first_ref[0, rows, cols] = one
+            second_ref[0, rows, cols] = two
+            step_ref[0, rows, cols] = (one / (jnp.sqrt(two) + epsilon)).astype(BF16)
 
     @pl.when(pl.program_id(0) == 0)
     def _():
@@ -535,7 +555,7 @@
         main_kernel,
         out_shape=(
             shape((ROWS, BACK), BF16),
-            shape((NE, 2, HID, LANE), BF16),
+            shape((2, NE, 2, HALF, LANE), BF16),
             shape((ROWS, TOK), BF16),
             shape((ROWS, TOK), BF16),
         ),
@@ -554,11 +574,12 @@
             pltpu.VMEM((HID, WIDTH), F32),
             pltpu.VMEM((WIDTH, 2 * HID), BF16),
             pltpu.VMEM((HID, WIDTH), BF16),
-            pltpu.VMEM((NE, 2, RAW, LANE), BF16),
-            pltpu.VMEM((NE, 2, RAW, LANE), BF16),
+            pltpu.VMEM((NE, 2, 2, RAW, LANE), BF16),
+            pltpu.VMEM((NE, 2, 2, RAW, LANE), BF16),
+            pltpu.VMEM((2, NE, POST, LANE), BF16),
             pltpu.VMEM((NE, POST, LANE), BF16),
             pltpu.VMEM((NE, POST, LANE), BF16),
-            pltpu.VMEM((NE, 2, HID, LANE), BF16),
+            pltpu.VMEM((2, NE, 2, HALF, LANE), BF16),
             pltpu.VMEM((ND, SLOTS, FEAT), BF16),
             pltpu.VMEM((NY, SLOTS, FEAT), BF16),
             pltpu.VMEM((NY, SLOTS, FEAT), BF16),
@@ -573,9 +594,11 @@
             pltpu.VMEM((ROWS, BACK), BF16),
             pltpu.VMEM((ROWS, ROWS), BF16),
             dma((9,)),
-            dma((5,)),
+            dma((7,)),
         ]
-        + [dma((NE,))] * 14
+        + [dma((NE,))] * 4
+        + [dma((2 * NE,))] * 4
+        + [dma((NE,))] * 6
         + [dma((NY,))] * 4,
         compiler_params=pltpu.CompilerParams(
             collective_id=0, has_side_effects=True, vmem_limit_bytes=VMEM_LIMIT
@@ -611,7 +634,7 @@
             shape((1, HID, WIDTH), BF16),
         ),
         in_specs=[
-            pl.BlockSpec((NE // steps, 2, HID, LANE), lambda i: (i, 0, 0, 0)),
+            pl.BlockSpec((2, NE // steps, 2, HALF, LANE), lambda i: (0, i, 0, 0, 0)),
             whole((ROWS, BACK)),
             whole((ROWS, TOK)),
             whole((ROWS, TOK)),

time: 182 us -> 177 us (0.973)
  Pallas kernels: 181 us -> 176 us
    pallas_call x1, Pallas kernels: 174 us -> 169 us  [per_device(): pl.pallas_call(main_kernel, out_shape=(shape((ROWS, BACK), BF16), shape((...]
where the time goes in v4:
time: 177 us; the launch traced here: 176 us
  Pallas kernels  176 us (99%)
    pallas_call x1, Pallas kernels, per_device(): pl.pallas_call(main_kernel, out_shape=(shape((ROWS, BACK), BF16), shape((...  169 us
    pallas_call x1, Pallas kernels, per_device(): pl.pallas_call(finish_kernel, grid=(steps,), out_shape=(shape((TOK, FEAT)...  7.29 us

profile of v4, /device:TPU:2, one launch (start us, length us, event | category | flops | bytes accessed | tf_op | source)
XLA Modules:
  0.0 176.5 jit_solution(8288978401111481199)
XLA Ops:
  0.6 168.6 %exchange.1 = (bf16[512,640]{1,0:T(8,128)(2,1)}, bf16[2,32,2,64,128]{4,3,2,1,0:T(8,128)(2,1)}, bf16[512,128]{1,0:T(8,128)(2,1)}, bf16[512,128]{1,0:T(8,128)(2,1)}) custom-call(s32[32]{0:T(128)} %previous_ref.1, s32[32]{0:T(128)} %next_ref.1, s32[4,128]{1,0:T(4,128)} %bitcast.2, f32[4,128]{1,0:T(4,128)} %bitcast.3, bf16[128,512]{1,0:T(8,128)(2,1)} %tok_hbm.1, ...), custom_call_target="tpu_custom_call" | custom-call | flops 4000000000 | bytes 16777216 | tf_op jit(solution)/shard_map/exchange/pallas_call | solution.py:554
  169.2 7.3 %finish.1 = (bf16[128,512]{1,0:T(8,128)(2,1)}, f32[1,128,4096]{2,1,0:T(8,128)}, f32[1,128,4096]{2,1,0:T(8,128)}, bf16[1,128,4096]{2,1,0:T(8,128)(2,1)}) custom-call(bf16[2,32,2,64,128]{4,3,2,1,0:T(8,128)(2,1)} %get-tuple-element.8.back_ref, bf16[512,640]{1,0:T(8,128)(2,1)} %get-tuple-element.9.ret_ref, bf16[512,128]{1,0:T(8,128)(2,1)} %get-tuple-element.10.main_ref, ...), custom_call_target="tpu_custom_call" | custom-call | flops 300000000 | bytes 8388608 | tf_op jit(solution)/shard_map/finish/pallas_call | solution.py:627
